TPU v7x, 256 devices: a whole 4x4x8 slice. The times are simulated.
256 devices in a mesh: section: 8 (over z_hi, core), row: 4 (over x), col: 8 (over y, z_lo).
Axes of the slice: x: 4, y: 4, z: 8 (z_hi: 4, z_lo: 2; z = z_hi * 2 + z_lo), core: 2. Of those that a mesh axis runs over, the one named last changes fastest.
Arguments:
- boundary_grad: bfloat16 [8, 1024, 12288], P('section', 'col', 'row'), may hold values from -6 to 6
- w_out: bfloat16 [8, 6144, 12288], P('section', 'col', 'row'), may hold values from -0.078125 to 0.078125
- context: bfloat16 [8, 1024, 6144], P('section', 'row', 'col'), may hold values from -6 to 6
- queries: bfloat16 [8, 1024, 6144], P('section', 'row', 'col'), may hold values from -24 to 24
- keys: bfloat16 [8, 1024, 6144], P('section', 'row', 'col'), may hold values from -24 to 24
- values: bfloat16 [8, 1024, 6144], P('section', 'row', 'col'), may hold values from -6 to 6
Outputs:
- grad_w_out: bfloat16 [8, 6144, 12288], P('section', 'col', 'row')
- grad_queries: bfloat16 [8, 1024, 6144], P('section', 'row', 'col')
- grad_keys: bfloat16 [8, 1024, 6144], P('section', 'row', 'col')
- grad_values: bfloat16 [8, 1024, 6144], P('section', 'row', 'col')
All inputs are finite; a program needn't handle non-finite values.
Results may differ from a plain program's by a relative error of at most 0.007.
Values may be sent and summed in bfloat16 or wider, within the bound.
A program may use at most 128 MiB of HBM per device.

v0:
```python
import jax
import jax.numpy as jnp
from jax import lax
from jax.sharding import PartitionSpec as P

HEAD_DIM = 128


def shifted(block, axis, distance):
    devices = range(lax.axis_size(axis))
    route = [(i - distance, i) for i in devices if i - distance in devices]
    return lax.ppermute(block, axis, route)


def attend_backward(query, key_rows, value_rows, output, grad_out, query_start):
    count = query.shape[0]
    total = key_rows.shape[0]
    heads = query.shape[1] // HEAD_DIM
    scale = HEAD_DIM ** (-0.5)
    qh = query.reshape(count, heads, HEAD_DIM)
    kh = key_rows.reshape(total, heads, HEAD_DIM)
    vh = value_rows.reshape(total, heads, HEAD_DIM)
    oh = output.reshape(count, heads, HEAD_DIM)
    gh = grad_out.reshape(count, heads, HEAD_DIM)
    scores = jnp.einsum("qhd,khd->hqk", qh, kh, preferred_element_type=jnp.float32) * scale
    query_pos = query_start + lax.broadcasted_iota(jnp.int32, (count, total), 0)
    key_pos = lax.broadcasted_iota(jnp.int32, (count, total), 1)
    allowed = query_pos >= key_pos
    scores = jnp.where(allowed[None], scores, -jnp.inf)
    top = jnp.max(scores, axis=2, keepdims=True)
    weights = jnp.exp(scores - top)
    probs = weights / jnp.sum(weights, axis=2, keepdims=True)
    delta = jnp.einsum("qhd,qhd->hq", gh.astype(jnp.float32), oh.astype(jnp.float32))
    dprobs = jnp.einsum("qhd,khd->hqk", gh, vh, preferred_element_type=jnp.float32)
    dscores = probs * (dprobs - delta[:, :, None])
    probs_b = probs.astype(jnp.bfloat16)
    dscores_b = dscores.astype(jnp.bfloat16)
    grad_v = jnp.einsum("hqk,qhd->khd", probs_b, gh, preferred_element_type=jnp.float32)
    grad_q = jnp.einsum("hqk,khd->qhd", dscores_b, kh, preferred_element_type=jnp.float32) * scale
    grad_k = jnp.einsum("hqk,qhd->khd", dscores_b, qh, preferred_element_type=jnp.float32) * scale
    width = heads * HEAD_DIM
    return (
        grad_q.reshape(count, width),
        grad_k.reshape(total, width),
        grad_v.reshape(total, width),
    )


def local(boundary_grad, w_out, context, queries, keys, values):
    later = shifted(boundary_grad, "section", -1)
    is_last = lax.axis_index("section") == lax.axis_size("section") - 1
    arriving = jnp.where(is_last, boundary_grad, later)[0]
    grad_rows = lax.all_gather(arriving, "col", axis=0, tiled=True)
    weight = w_out[0]
    own_context = context[0]
    own_query = queries[0]
    own_key = keys[0]
    own_value = values[0]
    rows = own_context.shape[0]
    row_start = lax.axis_index("row") * rows
    block = grad_rows
    grad_context = lax.psum_scatter(
        lax.dot_general(
            block, weight, (((1,), (1,)), ((), ())), preferred_element_type=jnp.float32
        ),
        "row",
        scatter_dimension=0,
        tiled=True,
    ).astype(jnp.bfloat16)
    key_all, value_all = (
        lax.all_gather(own_key, "row", axis=0, tiled=True),
        lax.all_gather(own_value, "row", axis=0, tiled=True),
    )
    block = grad_rows
    weight_grad = lax.dot_general(
        lax.all_gather(own_context, "row", axis=0, tiled=True),
        block,
        (((0,), (0,)), ((), ())),
        preferred_element_type=jnp.float32,
    )
    grad_q, partial_k, partial_v = attend_backward(
        own_query, key_all, value_all, own_context, grad_context, row_start
    )
    grad_k, grad_v = (
        lax.psum_scatter(partial_k, "row", scatter_dimension=0, tiled=True),
        lax.psum_scatter(partial_v, "row", scatter_dimension=0, tiled=True),
    )
    return (
        weight_grad.astype(jnp.bfloat16)[None],
        grad_q.astype(jnp.bfloat16)[None],
        grad_k.astype(jnp.bfloat16)[None],
        grad_v.astype(jnp.bfloat16)[None],
    )


def solution(mesh):
    in_specs = (
        P("section", "col", "row"),
        P("section", "col", "row"),
        P("section", "row", "col"),
        P("section", "row", "col"),
        P("section", "row", "col"),
        P("section", "row", "col"),
    )
    out_specs = (
        P("section", "col", "row"),
        P("section", "row", "col"),
        P("section", "row", "col"),
        P("section", "row", "col"),
    )
    return jax.shard_map(local, mesh=mesh, in_specs=in_specs, out_specs=out_specs, check_vma=False)
```

profile of v0, /device:TPU:1, one launch (start us, length us, event | category | flops | bytes accessed | tf_op | source)
XLA Modules:
  0.0 409.1 jit_solution(12631634009259470436)
XLA Ops:
  7.2 0.0 copy-start.5
  7.2 0.0 all-gather.9.cloned.1.call-start
  7.2 5.3 %collective-permute-start = (bf16[1,128,3072]{2,1,0:T(8,128)(2,1)}, bf16[1,128,3072]{2,1,0:T(8,128)(2,1)S(1)}, u32[]{:S(2)}, u32[]{:S(2)}) collective-permute-start(bf16[1,128,3072]{2,1,0:T(8,128)(2,1)} %param.6), channel_id=1, source_target_pairs={{32,0},{64,32},{96,64},{128,96},{160,128},{192,160},{224,192},{33,... | collective-permute-start | bytes 2359304 | tf_op jit(solution)/shard_map/ppermute | solution.py:12
  12.5 19.4 %collective-permute-done = bf16[1,128,3072]{2,1,0:T(8,128)(2,1)S(1)} collective-permute-done((bf16[1,128,3072]{2,1,0:T(8,128)(2,1)}, bf16[1,128,3072]{2,1,0:T(8,128)(2,1)S(1)}, u32[]{:S(2)}, u32[]{:S(2)}) %collective-permute-start) | collective-permute-done | bytes 786464 | tf_op jit(solution)/shard_map/ppermute | solution.py:12
  31.9 1.0 broadcast_select_fusion
  32.9 0.0 all-gather.9.cloned.1.call-update
  32.9 0.0 all-gather.13.cloned.1.call-start
  33.0 0.0 copy-done.5
  33.0 0.9 copy.20
  33.9 0.0 all-gather.13.cloned.1.call-update
  33.9 0.0 reduce-scatter.4.cloned.1.call-start
  34.0 132.4 %all-gather.9.cloned.1.call-done = bf16[1,1024,3072]{2,1,0:T(8,128)(2,1)} async-done(((bf16[1,128,3072]{2,1,0:T(8,128)(2,1)}), bf16[1,1024,3072]{2,1,0:T(8,128)(2,1)}) %all-gather.9.cloned.1.call-update) | async-done | bytes 6291472 | tf_op jit(solution)/shard_map/all_gather | solution.py:53
  166.4 9.7 %fusion.1 = f32[1024,768]{1,0:T(8,128)} fusion(bf16[1,1024,3072]{2,1,0:T(8,128)(2,1)} %all-gather.9.cloned.1.call-done, bf16[1,768,3072]{2,1,0:T(8,128)(2,1)} %param.7), kind=kOutput, calls=%fused_computation.1 | convolution fusion | flops 4831838208 | bytes 14155776 | tf_op jit(solution)/shard_map/dot_general | solution.py:63
  176.1 0.0 copy-start.6
  176.1 0.0 copy-start.2
  176.1 0.0 copy-start.7
  176.1 0.0 reduce-scatter.4.cloned.1.call-update
  176.1 0.0 all-gather.15.cloned.1.call-start
  176.2 0.9 copy-done.6
  177.1 0.9 copy.24
  178.0 0.0 all-gather.15.cloned.1.call-update
  178.0 0.0 all-gather.11.cloned.1.call-start
  178.1 0.5 all-gather.11.cloned.1.call-update
  178.6 0.0 reduce-scatter.6.cloned.1.call-start
  178.7 0.0 copy-done.2
  178.7 0.2 copy.44
  178.9 0.0 copy-done.7
  178.9 0.2 copy.19
  179.1 0.2 iota_compare_fusion
  179.3 22.2 %all-gather.13.cloned.1.call-done = bf16[1,1024,768]{1,2,0:T(8,128)(2,1)} async-done(((bf16[1,256,768]{1,2,0:T(8,128)(2,1)}), bf16[1,1024,768]{1,2,0:T(8,128)(2,1)}) %all-gather.13.cloned.1.call-update) | async-done | bytes 1572880 | tf_op jit(solution)/shard_map/all_gather | solution.py:71
  201.5 6.4 %fusion.25 = (f32[6,256]{1,0:T(8,128)S(1)}, f32[6,256,1024]{2,1,0:T(8,128)}) fusion(pred[256,1024]{1,0:T(8,128)(4,1)S(1)} %iota_compare_fusion, bf16[256,6,128]{0,2,1:T(8,128)(2,1)S(1)} %bitcast.57, bf16[1024,6,128]{0,2,1:T(8,128)(2,1)} %bitcast.64), kind=kOutput, calls=%fused_computation.32 | convolution fusion | flops 408945664 | bytes 8525824 | tf_op jit(solution)/shard_map/sub | solution.py:31
  207.9 39.4 %reduce-scatter.4.cloned.1.call-done = f32[256,768]{1,0:T(8,128)} async-done(((f32[1024,768]{1,0:T(8,128)}), f32[256,768]{1,0:T(8,128)}) %reduce-scatter.4.cloned.1.call-update) | async-done | bytes 786448 | tf_op jit(solution)/shard_map/reduce_scatter | solution.py:62
  247.4 1.2 convert_element_type.41
  248.5 0.2 copy.23
  248.7 0.0 copy-start.3
  248.7 0.1 fusion.20
  248.8 32.3 %all-gather.15.cloned.1.call-done = bf16[1,1024,768]{1,2,0:T(8,128)(2,1)} async-done(((bf16[1,256,768]{1,2,0:T(8,128)(2,1)}), bf16[1,1024,768]{1,2,0:T(8,128)(2,1)}) %all-gather.15.cloned.1.call-update) | async-done | bytes 1572880 | tf_op jit(solution)/shard_map/all_gather | solution.py:72
  281.2 0.0 copy-done.3
  281.2 4.1 multiply_convert_fusion
  285.3 0.0 copy-start
  285.3 0.7 convolution_multiply_fusion
  285.9 1.0 copy-done
  286.9 2.4 copy.28
  289.3 0.0 copy-start.4
  289.3 0.0 reduce-scatter.6.cloned.1.call-update
  289.3 0.2 reduce-scatter.8.cloned.1.call-start
  289.5 0.7 copy-done.4
  290.3 3.6 fusion.13
  293.9 2.4 copy.29
  296.3 0.0 reduce-scatter.8.cloned.1.call-update
  296.3 17.5 %all-gather.11.cloned.1.call-done = bf16[1,1024,768]{2,1,0:T(8,128)(2,1)} async-done(((bf16[1,256,768]{2,1,0:T(8,128)(2,1)}), bf16[1,1024,768]{2,1,0:T(8,128)(2,1)}) %all-gather.11.cloned.1.call-update) | async-done | bytes 1572880 | tf_op jit(solution)/shard_map/all_gather | solution.py:76
  313.8 9.1 %fusion.10 = bf16[1,768,3072]{1,2,0:T(8,128)(2,1)} fusion(bf16[1,1024,3072]{2,1,0:T(8,128)(2,1)} %all-gather.9.cloned.1.call-done, bf16[1,1024,768]{2,1,0:T(8,128)(2,1)} %all-gather.11.cloned.1.call-done), kind=kOutput, calls=%fused_computation.11 | convolution fusion | flops 4834197504 | bytes 12582912 | tf_op jit(solution)/shard_map/dot_general | solution.py:75
  322.9 0.0 copy-start.1
  322.9 7.0 %copy.30 = bf16[1,768,3072]{2,1,0:T(8,128)(2,1)} copy(bf16[1,768,3072]{1,2,0:T(8,128)(2,1)} %fusion.10) | data formatting | bytes 9437184
  329.9 0.0 copy-done.1
  329.9 2.6 fusion.19
  332.5 0.9 copy.31
  333.4 23.7 %reduce-scatter.6.cloned.1.call-done = f32[256,768]{1,0:T(8,128)} async-done(((f32[1024,768]{1,0:T(8,128)}), f32[256,768]{1,0:T(8,128)}) %reduce-scatter.6.cloned.1.call-update) | async-done | bytes 786448 | tf_op jit(solution)/shard_map/reduce_scatter | solution.py:85
  357.2 1.9 convert_bitcast_fusion.1
  359.1 41.2 %reduce-scatter.8.cloned.1.call-done = f32[256,768]{1,0:T(8,128)} async-done(((f32[1024,768]{1,0:T(8,128)}), f32[256,768]{1,0:T(8,128)}) %reduce-scatter.8.cloned.1.call-update) | async-done | bytes 786448 | tf_op jit(solution)/shard_map/reduce_scatter | solution.py:86
  400.3 1.9 convert_bitcast_fusion
  (1 shorter events, 0.0 us)
Async XLA Ops:
  7.2 25.8 %copy-start.5 = (bf16[1,256,768]{2,1,0:T(8,128)(2,1)S(1)}, bf16[1,256,768]{2,1,0:T(8,128)(2,1)}, u32[]{:S(2)}) copy-start(bf16[1,256,768]{2,1,0:T(8,128)(2,1)} %param.10) | copy-start | bytes 1179652
  7.2 159.2 %all-gather.9.cloned.1.call-start = ((), (), s32[]{:S(2)}) async-start(), calls=%async_computation.6 | async-start | bytes 7077888 | tf_op jit(solution)/shard_map/all_gather | solution.py:53
  7.2 24.7 %collective-permute-start = (bf16[1,128,3072]{2,1,0:T(8,128)(2,1)}, bf16[1,128,3072]{2,1,0:T(8,128)(2,1)S(1)}, u32[]{:S(2)}, u32[]{:S(2)}) collective-permute-start(bf16[1,128,3072]{2,1,0:T(8,128)(2,1)} %param.6), channel_id=1, source_target_pairs={{32,0},{64,32},{96,64},{128,96},{160,128},{192,160},{224,192},{33,... | collective-permute-start | bytes 2359304 | tf_op jit(solution)/shard_map/ppermute | solution.py:12
  32.9 168.5 %all-gather.13.cloned.1.call-start = ((), (), s32[]{:S(2)}) async-start(), calls=%async_computation.8 | async-start | bytes 1966080 | tf_op jit(solution)/shard_map/all_gather | solution.py:71
  33.9 213.4 %reduce-scatter.4.cloned.1.call-start = ((), (), s32[]{:S(2)}) async-start(), calls=%async_computation.3 | async-start | bytes 3932160 | tf_op jit(solution)/shard_map/reduce_scatter | solution.py:62
  176.1 1.0 copy-start.6
  176.1 2.6 copy-start.2
  176.1 2.8 copy-start.7
  176.1 105.0 %all-gather.15.cloned.1.call-start = ((), (), s32[]{:S(2)}) async-start(), calls=%async_computation.9 | async-start | bytes 1966080 | tf_op jit(solution)/shard_map/all_gather | solution.py:72
  178.0 135.8 %all-gather.11.cloned.1.call-start = ((), (), s32[]{:S(2)}) async-start(), calls=%async_computation.7 | async-start | bytes 1966080 | tf_op jit(solution)/shard_map/all_gather | solution.py:76
  178.6 178.6 %reduce-scatter.6.cloned.1.call-start = ((), (), s32[]{:S(2)}) async-start(), calls=%async_computation.4 | async-start | bytes 3932160 | tf_op jit(solution)/shard_map/reduce_scatter | solution.py:85
  248.7 32.5 %copy-start.3 = (bf16[256,768]{0,1:T(8,128)(2,1)}, bf16[256,768]{0,1:T(8,128)(2,1)S(1)}, u32[]{:S(2)}) copy-start(bf16[256,768]{0,1:T(8,128)(2,1)S(1)} %copy.23) | copy-start | bytes 1179652
  285.3 1.7 copy-start
  289.3 1.0 copy-start.4
  289.3 111.0 %reduce-scatter.8.cloned.1.call-start = ((), (), s32[]{:S(2)}) async-start(), calls=%async_computation.5 | async-start | bytes 3932160 | tf_op jit(solution)/shard_map/reduce_scatter | solution.py:86
  322.9 7.0 %copy-start.1 = (bf16[6,256,1024]{2,1,0:T(8,128)(2,1)S(1)}, bf16[6,256,1024]{2,1,0:T(8,128)(2,1)}, u32[]{:S(2)}) copy-start(bf16[6,256,1024]{2,1,0:T(8,128)(2,1)} %copy-done) | copy-start | bytes 9437188
Sparse Core Ops, SparseCore 0:
  33.1 133.2 all-gather.8
  168.7 32.6 all-gather.12
  204.6 42.7 reduce-scatter.3
  249.6 31.5 all-gather.14
  282.8 30.9 all-gather.10
  316.2 40.9 reduce-scatter.5
  359.7 40.5 reduce-scatter.7
where the time goes:
time: 410 us; the launch traced here: 409 us
  waiting for transfers between devices  329 us (80%)
  matrix products  36.3 us (9%)
  local copies, waits for them, and re-layouts  17.6 us (4%)
  between operations  14.3 us (3%)
  other arithmetic  6.31 us (2%)
  starting transfers between devices  5.75 us (1%)
    all_gather x1, waiting for transfers between devices, local(): grad_rows = lax.all_gather(arriving, 'col', axis=0, tiled=True)  132 us
    reduce_scatter x1, waiting for transfers between devices, local(): lax.psum_scatter(partial_v, 'row', scatter_dimension=0, tiled=True)  41.2 us
    reduce_scatter x1, waiting for transfers between devices, local(): lax.psum_scatter(lax.dot_general(block, weight, (((1,), (1,)), ((), ())),...  39.4 us
    all_gather x1, waiting for transfers between devices, local(): lax.all_gather(own_value, 'row', axis=0, tiled=True)  32.3 us
    reduce_scatter x1, waiting for transfers between devices, local(): lax.psum_scatter(partial_k, 'row', scatter_dimension=0, tiled=True)  23.7 us
    all_gather x1, waiting for transfers between devices, local(): lax.all_gather(own_key, 'row', axis=0, tiled=True)  22.2 us
    ppermute x1, waiting for transfers between devices, shifted(): return lax.ppermute(block, axis, route)  19.4 us
    all_gather x1, waiting for transfers between devices, local(): lax.all_gather(own_context, 'row', axis=0, tiled=True)  17.5 us
  transfers between devices with their start and end apart: 8, of which 8 were waited for; matrix products, arithmetic and copies ran while one was open for 13% of the time, Pallas kernels for 0%

commit v1 on v0

v1 whole, which is shorter than its diff:
```python
import jax
import jax.numpy as jnp
from jax import lax
from jax.experimental import pallas as pl
from jax.experimental.pallas import tpu as pltpu
from jax.sharding import PartitionSpec as P

HEAD = 128
SCALE = HEAD ** (-0.5)
MESH = pl.DeviceIdType.MESH
BF16 = jnp.bfloat16
F32 = jnp.float32

ROWS = 256
PIECE = 128
HALF = 64
KEYS = 512
FEAT = 3072
WIDTH = 768
PAIR = 384
SLAB = 256
TILE = 512

ORDER0 = [
    "E1", "E0", "e0l", "q", "e0r", "k", "e1l", "cB", "e1r", "cA", "kf", "f0", "f1", "qf", "cfB", "zs1", "P0", "P1",
    "cfA", "zs0", "t0", "p0", "g0a", "zr1", "t1", "zr1r", "P2", "v", "zr0l", "t2", "s0", "g0b", "f3", "vf", "zr0",
    "p1", "f2", "t3", "P3", "a0", "s1", "p2", "g1a", "p3", "g1b", "s2", "a1", "g2a", "g2b", "dq", "s3", "a2", "g3a",
    "dqf", "g3b", "a3", "dk", "dv", "dql",
]
ORDER1 = [
    "E1", "q", "cB", "E0", "e0l", "e0r", "k", "cA", "e1l", "e1r", "kf", "f0", "f1", "qf", "zs1", "P0", "cfB", "P1",
    "cfA", "zs0", "t0", "p0", "zr1r", "g0a", "zr1", "t1", "v", "P2", "zr0l", "s0", "g0b", "f3", "zr0", "p1", "t2",
    "f2", "vf", "P3", "a0", "s1", "p2", "g1a", "p3", "g1b", "s2", "t3", "a1", "g2a", "g2b", "dq", "s3", "a2", "g3a",
    "dqf", "g3b", "a3", "dk", "dv", "dql",
]


def dot(a, b, ca, cb):
    return lax.dot_general(a, b, (((ca,), (cb,)), ((), ())), preferred_element_type=F32)


def kernel(
    bg, wo, cx, qs, ks, vs,
    gw, gq, gk, gv,
    inc, wv, ctx, ctxt, acc, q2, k2, v2, qg, part, partb, got_a, got_b, sumb, pt, linv, dout,
    dqa, dka, dva, dqb, dkb, dvb, stage,
    send, recv, lsem, esem, osem,
):
    s = lax.axis_index("section")
    x = lax.axis_index("row")
    c = lax.axis_index("col")
    y = c // 2
    z = c - 2 * y
    core = s - 2 * (s // 2)
    y_r = lax.rem(y + 1 + 2 * core, 4)
    y_l = lax.rem(y + 3 + 2 * core, 4)
    y_o = lax.rem(y + 2, 4)
    zp = 1 - z
    pair = x // 2
    par = x - 2 * pair
    par_b = 1 - par
    x_a = 3 - x
    x_b = 2 * pair + par_b
    x_c = lax.rem(x + 2, 4)
    dev_r = (s, x, 2 * y_r + z)
    dev_l = (s, x, 2 * y_l + z)
    dev_z = (s, x, 2 * y + zp)
    dev_a = (s, x_a, c)
    dev_b = (s, x_b, c)
    has_prev = s > 0
    has_next = s < 7
    dev_prev = (jnp.maximum(s - 1, 0), x, c)
    dev_next = (jnp.minimum(s + 1, 7), x, c)

    barrier = pltpu.get_barrier_semaphore()
    for dev in (dev_r, dev_l, dev_z, dev_a, dev_b):
        pl.semaphore_signal(barrier, inc=1, device_id=dev, device_id_type=MESH)

    @pl.when(has_prev)
    def _():
        pl.semaphore_signal(barrier, inc=1, device_id=dev_prev, device_id_type=MESH)

    @pl.when(has_next)
    def _():
        pl.semaphore_signal(barrier, inc=1, device_id=dev_next, device_id_type=MESH)

    pl.semaphore_wait(barrier, 5 + has_prev.astype(jnp.int32) + has_next.astype(jnp.int32))

    def m128(v):
        return pl.multiple_of(v, 128)

    def slab_of(xx):
        p = xx // 2
        return pl.ds(m128(PAIR * p + HEAD * (xx - 2 * p)), SLAB)

    def full_of(xx):
        p = xx // 2
        return pl.ds(m128(PAIR * p + 2 * HEAD * (xx - 2 * p)), HEAD)

    def pair_of(xx):
        return pl.ds(m128(PAIR * (xx // 2)), PAIR)

    own_slab = slab_of(x)
    in_pair = pl.ds(m128(HEAD * par), SLAB)
    in_pair_b = pl.ds(m128(HEAD * par_b), SLAB)
    own_full = pl.ds(m128(HEAD * par), HEAD)

    def slot(yy, zz, h):
        half = yy // 2
        return inc.at[2 * zz + half, pl.ds(pl.multiple_of(PIECE * (yy - 2 * half) + HALF * h, HALF), HALF)]

    groups = [2 * z + y // 2, 2 * z + 1 - y // 2, 2 * zp + y // 2, 2 * zp + 1 - y // 2]

    moves = {}

    def move(tag, src, there, here, dev):
        moves[tag] = (len(moves), src, there, here, dev)

    for h in range(2):
        move("E%d" % h, bg.at[0, pl.ds(HALF * h, HALF)], slot(y, z, h), slot(y, z, h), dev_prev)
        move("z%d" % h, slot(y, z, h), slot(y, z, h), slot(y, zp, h), dev_z)
        move("l_own%d" % h, slot(y, z, h), slot(y, z, h), slot(y_l, z, h), dev_r)
        move("r_own%d" % h, slot(y, z, h), slot(y, z, h), slot(y_r, z, h), dev_l)
        move("l_oth%d" % h, slot(y, zp, h), slot(y, zp, h), slot(y_l, zp, h), dev_r)
        move("r_oth%d" % h, slot(y, zp, h), slot(y, zp, h), slot(y_r, zp, h), dev_l)
    move("o_own0", slot(y_l, z, 0), slot(y_l, z, 0), slot(y_o, z, 0), dev_r)
    move("o_own1", slot(y_r, z, 1), slot(y_r, z, 1), slot(y_o, z, 1), dev_l)
    move("o_oth1", slot(y_r, zp, 1), slot(y_r, zp, 1), slot(y_o, zp, 1), dev_l)
    move("o_oth0", slot(y_o, z, 0), slot(y_o, z, 0), slot(y_o, zp, 0), dev_z)
    def block(xx, start=0, size=ROWS):
        half = xx // 2
        return half, pl.ds(m128(ROWS * (xx - 2 * half) + start), size)

    for n, a, b in (("k", ks, k2), ("q", qs, q2), ("v", vs, v2)):
        to, from_a, from_b, from_c = block(x), block(x_a), block(x_b), block(x_c)
        move(n + "A", a.at[0, :, pair_of(x_a)], b.at[to], b.at[from_a], dev_a)
        move(n + "B", a.at[0, :, slab_of(x_b)], b.at[(*to, in_pair_b)], b.at[(*from_b, in_pair)], dev_b)
        move(n + "C", b.at[(*from_a, in_pair_b)], b.at[(*from_a, in_pair_b)], b.at[(*from_c, in_pair)], dev_b)
    move("cA", cx.at[0], ctx.at[x], ctx.at[x_a], dev_a)
    move("cB", cx.at[0], ctx.at[x], ctx.at[x_b], dev_b)
    lo, hi = pl.ds(0, ROWS // 2), pl.ds(ROWS // 2, ROWS // 2)
    move("cC0", ctx.at[x_a, lo], ctx.at[x_a, lo], ctx.at[x_c, lo], dev_b)
    move("cC1", ctx.at[x_b, hi], ctx.at[x_b, hi], ctx.at[x_c, hi], dev_a)
    for k in range(4):
        move("rsA%d" % k, partb.at[k, :, pair_of(x_a)], got_a.at[k], got_a.at[k], dev_a)
        move("rsB%d" % k, sumb.at[k], got_b.at[k], got_b.at[k], dev_b)

    def move_out(n, src, dst, start, size, where):
        rows = pl.ds(start, size)
        hop = stage.at[where, pl.ds(0, size)]
        to_a, to_b, to_c = (block(xx, start, size) for xx in (x_a, x_b, x_c))
        move(n + "1", src.at[(*to_c, own_full)], hop, hop, dev_b)
        move(n + "A", src.at[to_a], dst.at[0, rows, own_slab], dst.at[0, rows, slab_of(x_a)], dev_a)
        move(n + "B", src.at[(*to_b, own_full)], dst.at[0, rows, full_of(x)], dst.at[0, rows, full_of(x_b)], dev_b)
        move(n + "C", hop, dst.at[0, rows, full_of(x_b)], dst.at[0, rows, full_of(x_c)], dev_a)

    move_out("dk", dkb, gk, 0, ROWS, 0)
    move_out("dv", dvb, gv, 0, ROWS, 1)
    move_out("dqe", dqb, gq, m128(PIECE * z), PIECE, 2)
    move_out("dql", dqb, gq, m128(PIECE * zp), PIECE, 3)

    def outgoing(tag):
        i, src, there, _, dev = moves[tag]
        return pltpu.make_async_remote_copy(src, there, send.at[i], recv.at[i], device_id=dev, device_id_type=MESH)

    def arriving(tag):
        i, _, _, here, dev = moves[tag]
        return pltpu.make_async_remote_copy(here, here, send.at[i], recv.at[i], device_id=dev, device_id_type=MESH)

    def entry_kept(h):
        return pltpu.make_async_copy(bg.at[0, pl.ds(HALF * h, HALF)], slot(y, z, h), esem.at[h])

    loads = []
    for src, dst in (
        (ks.at[0, :, own_slab], k2.at[(*block(x), in_pair)]),
        (qs.at[0, :, own_slab], q2.at[(*block(x), in_pair)]),
        (vs.at[0, :, own_slab], v2.at[(*block(x), in_pair)]),
        (cx.at[0], ctx.at[x]),
        (wo.at[0], wv),
    ):
        loads.append(pltpu.make_async_copy(src, dst, lsem.at[len(loads)]))

    def emit_send(tag):
        if tag[0] == "E":
            h = int(tag[1])

            @pl.when(has_prev)
            def _():
                outgoing(tag).start()

            @pl.when(jnp.logical_not(has_next))
            def _():
                entry_kept(h).start()
        else:
            outgoing(tag).start()

    def emit_wait(tag):
        if tag[0] == "E":
            h = int(tag[1])

            @pl.when(has_next)
            def _():
                arriving(tag).wait_recv()

            @pl.when(jnp.logical_not(has_next))
            def _():
                entry_kept(h).wait()
        elif tag[0] == "@":
            loads[int(tag[1])].wait()
        else:
            arriving(tag).wait_recv()

    def group_rows(g):
        zz = g // 2
        return g - 2 * zz, zz, pl.ds(m128(PIECE * zz), PIECE), pl.ds(m128(ROWS + PIECE * zz), PIECE)

    def partial_grad(k):
        g = groups[k]

        @pl.loop(0, 3)
        def _(n):
            rows = pl.ds(pl.multiple_of(n * 256, 256), 256)
            r = dot(inc[g], wv[rows], 1, 1)
            part[k, :, rows] = r
            partb[k, :, rows] = r.astype(BF16)

    def pass_on(k):
        r = part[k, :, slab_of(x_b)] + got_a[k, :, in_pair_b].astype(F32)
        sumb[k] = r.astype(BF16)

    heads = [pl.ds(HEAD * h, HEAD) for h in range(2)]
    pheads = [pl.ds(m128(HEAD * (par + h)), HEAD) for h in range(2)]

    def softmax(k):
        p, zz, rows0, rows1 = group_rows(groups[k])
        row = lax.broadcasted_iota(jnp.int32, (KEYS, ROWS), 0)
        lane = lax.broadcasted_iota(jnp.int32, (KEYS, ROWS), 1)
        ahead = jnp.where(lane < PIECE, lane, lane + PIECE) - row
        for h in range(2):
            qg[k, 0:PIECE, heads[h]] = q2[p, rows0, pheads[h]]
            qg[k, PIECE:ROWS, heads[h]] = q2[p, rows1, pheads[h]]

        def scores(j, tops):
            result = []
            ok = ahead >= KEYS * (j - p) - PIECE * zz
            for h in range(2):
                sc = dot(k2[j, :, pheads[h]], qg[k, :, heads[h]], 1, 1) * SCALE
                sc = jnp.where(ok, sc, -jnp.inf)
                pt[h, k, j] = sc
                result.append(jnp.maximum(tops[h], jnp.max(sc, axis=0, keepdims=True)))
            return tuple(result)

        low = jnp.full((1, ROWS), -jnp.inf, F32)
        tops = lax.fori_loop(0, p + 1, scores, (low, low))

        def weights(j, sums):
            result = []
            for h in range(2):
                e = jnp.exp(pt[h, k, j] - tops[h])
                pt[h, k, j] = e
                result.append(sums[h] + jnp.sum(e, axis=0, keepdims=True))
            return tuple(result)

        none = jnp.zeros((1, ROWS), F32)
        sums = lax.fori_loop(0, p + 1, weights, (none, none))
        for h in range(2):
            linv[k, h : h + 1] = 1.0 / sums[h]

    def turn(k):
        p, _, rows, _ = group_rows(groups[k])
        ctxt[k, :, 0:PIECE] = ctx[2 * p, rows].T
        ctxt[k, :, PIECE:ROWS] = ctx[2 * p + 1, rows].T

    def weight_grad(k, half, first):
        g = groups[k]

        @pl.loop(0, FEAT // TILE // 2)
        def _(n):
            cols = pl.ds(pl.multiple_of(half * (FEAT // 2) + n * TILE, TILE), TILE)
            r = dot(ctxt[k], inc[g, :, cols], 1, 0)
            if not first:
                r = r + acc[:, cols]
            if k == 3:
                gw[0, :, cols] = r.astype(BF16)
            else:
                acc[:, cols] = r

    def attend(k):
        p, _, rows0, rows1 = group_rows(groups[k])
        if k == 0:
            dka[...] = jnp.zeros_like(dka)
            dva[...] = jnp.zeros_like(dva)
        grad = part[k, :, own_slab] + got_a[k, :, in_pair].astype(F32) + got_b[k].astype(F32)
        gb = grad.astype(BF16)
        dout[...] = gb
        rounded = gb.astype(F32)
        top = (rounded[0:PIECE] * ctx[2 * p, rows0, own_slab].astype(F32)).T
        low = (rounded[PIECE:ROWS] * ctx[2 * p + 1, rows0, own_slab].astype(F32)).T
        deltas = []
        for h in range(2):
            sel = slice(HEAD * h, HEAD * (h + 1))
            deltas.append(
                jnp.concatenate(
                    [jnp.sum(top[sel], axis=0, keepdims=True), jnp.sum(low[sel], axis=0, keepdims=True)], axis=1
                )
            )
        inv = [linv[k, h : h + 1] for h in range(2)]
        dqa[...] = jnp.zeros_like(dqa)

        @pl.loop(0, p + 1)
        def _(j):
            for h in range(2):
                gh = dout[:, heads[h]]
                w = pt[h, k, j] * inv[h]
                dp = dot(v2[j, :, pheads[h]], gh, 1, 1)
                ds = (w * (dp - deltas[h])).astype(BF16)
                dva[j, :, heads[h]] += dot(w.astype(BF16), gh, 1, 0)
                dka[j, :, heads[h]] += dot(ds, qg[k, :, heads[h]], 1, 0)
                dqa[:, heads[h]] += dot(ds, k2[j, :, pheads[h]], 0, 0)

        dqb[p, rows0] = (dqa[0:PIECE] * SCALE).astype(BF16)
        dqb[p, rows1] = (dqa[PIECE:ROWS] * SCALE).astype(BF16)

    def cast_keys():
        dkb[...] = (dka[...] * SCALE).astype(BF16)

    def cast_values():
        dvb[...] = dva[...].astype(BF16)

    table = {
        "E0": ([], None, ["E0"]),
        "E1": ([], None, ["E1"]),
        "cA": ([], None, ["cA"]),
        "cB": ([], None, ["cB"]),
        "cfA": (["cA"], None, ["cC0"]),
        "cfB": (["cB"], None, ["cC1"]),
        "e0r": (["E0"], None, ["l_own0"]),
        "e0l": (["E0"], None, ["r_own0"]),
        "e1l": (["E1"], None, ["r_own1"]),
        "e1r": (["E1"], None, ["l_own1"]),
        "zs0": (["E0"], None, ["z0"]),
        "zs1": (["E1"], None, ["z1"]),
        "f0": (["l_own0"], None, ["o_own0"]),
        "f1": (["r_own1"], None, ["o_own1"]),
        "f2": (["r_oth1"], None, ["o_oth1"]),
        "f3": (["o_own0"], None, ["o_oth0"]),
        "zr0": (["z0"], None, ["l_oth0"]),
        "zr0l": (["z0"], None, ["r_oth0"]),
        "zr1": (["z1"], None, ["r_oth1"]),
        "zr1r": (["z1"], None, ["l_oth1"]),
        "dq": ([], None, ["dqe1", "dqeA", "dqeB"]),
        "dqf": (["dqe1"], None, ["dqeC"]),
        "dk": ([], cast_keys, ["dk1", "dkA", "dkB"]),
        "dv": ([], cast_values, ["dv1", "dvA", "dvB"]),
        "dql": ([], None, ["dql1", "dqlA", "dqlB"]),
    }
    own = ["E0", "E1"]
    near = ["l_own0", "l_own1", "r_own0", "r_own1"]
    far = ["o_own0", "o_own1"]
    near_z = ["z0", "z1", "l_oth0", "l_oth1", "r_oth0", "r_oth1"]
    far_z = ["o_oth0", "o_oth1"]
    for n in "kqv":
        table[n] = ([], None, [n + "A", n + "B"])
        table[n + "f"] = ([n + "A"], None, [n + "C"])
    for k, need in enumerate((["@4"] + own + near, far, near_z, far_z)):
        table["p%d" % k] = (need, lambda k=k: partial_grad(k), ["rsA%d" % k])
        table["s%d" % k] = (["rsA%d" % k], lambda k=k: pass_on(k), ["rsB%d" % k])
        table["P%d" % k] = (["@0", "@1", "kA", "kB", "kC", "qA", "qB", "qC"], lambda k=k: softmax(k), [])
        table["t%d" % k] = (["@3", "cA", "cB", "cC0", "cC1"], lambda k=k: turn(k), [])
        table["a%d" % k] = (["@2", "vA", "vB", "vC", "rsB%d" % k], lambda k=k: attend(k), [])

    def perform(order):
        seen = set()
        touched = set()
        for name in order:
            if name[0] == "g":
                k, half = int(name[1]), "ab".index(name[2])
                weight_grad(k, half, half not in touched)
                touched.add(half)
                continue
            waits, work, sends = table[name]
            for tag in waits:
                if tag not in seen:
                    seen.add(tag)
                    emit_wait(tag)
            if work is not None:
                work()
            for tag in sends:
                emit_send(tag)
        for n, (b, g) in enumerate(((dqb, gq), (dkb, gk), (dvb, gv))):
            pltpu.make_async_copy(b.at[block(x)], g.at[0, :, own_slab], osem.at[n]).start()
        for n in ("dk", "dv", "dql"):
            emit_wait(n + "1")
            emit_send(n + "C")

    for copy in loads:
        copy.start()
    for n, order in enumerate((ORDER0, ORDER1)):
        pl.when(core == n)(lambda order=order: perform(order))

    for n in ("dqe", "dk", "dv", "dql"):
        for tail in "ABC":
            emit_wait(n + tail)
    for n, (b, g) in enumerate(((dqb, gq), (dkb, gk), (dvb, gv))):
        pltpu.make_async_copy(b.at[block(x)], g.at[0, :, own_slab], osem.at[n]).wait()
    for tag in moves:
        if tag[0] == "E":

            @pl.when(has_prev)
            def _():
                outgoing(tag).wait_send()
        else:
            outgoing(tag).wait_send()


N_MOVES = 2 * 6 + 4 + 9 + 4 + 8 + 16


def write_out(gw, gq, gk, gv, gw_out, gq_out, gk_out, gv_out, sems):
    copies = []
    for n in range(6):
        rows = pl.ds(n * (WIDTH // 6), WIDTH // 6)
        copies.append(pltpu.make_async_copy(gw.at[0, rows], gw_out.at[0, rows], sems.at[n]))
    for n, (src, dst) in enumerate(((gq, gq_out), (gk, gk_out), (gv, gv_out))):
        copies.append(pltpu.make_async_copy(src, dst, sems.at[6 + n]))
    for copy in copies:
        copy.start()
    for copy in copies:
        copy.wait()


def local(boundary_grad, w_out, context, queries, keys, values):
    any_spec = pl.BlockSpec(memory_space=pl.ANY)
    vmem_spec = pl.BlockSpec(memory_space=pltpu.VMEM)
    shapes = [(1, WIDTH, FEAT), (1, ROWS, WIDTH), (1, ROWS, WIDTH), (1, ROWS, WIDTH)]
    grads = pl.pallas_call(
        kernel,
        out_shape=[pltpu.VMEM(shape, BF16) for shape in shapes],
        in_specs=[any_spec] * 6,
        out_specs=[vmem_spec] * 4,
        scratch_shapes=[
            pltpu.VMEM((4, ROWS, FEAT), BF16),
            pltpu.VMEM((WIDTH, FEAT), BF16),
            pltpu.VMEM((4, ROWS, WIDTH), BF16),
            pltpu.VMEM((4, WIDTH, ROWS), BF16),
            pltpu.VMEM((WIDTH, FEAT), F32),
            pltpu.VMEM((2, KEYS, PAIR), BF16),
            pltpu.VMEM((2, KEYS, PAIR), BF16),
            pltpu.VMEM((2, KEYS, PAIR), BF16),
            pltpu.VMEM((4, ROWS, SLAB), BF16),
            pltpu.VMEM((4, ROWS, WIDTH), F32),
            pltpu.VMEM((4, ROWS, WIDTH), BF16),
            pltpu.VMEM((4, ROWS, PAIR), BF16),
            pltpu.VMEM((4, ROWS, SLAB), BF16),
            pltpu.VMEM((4, ROWS, SLAB), BF16),
            pltpu.VMEM((2, 4, 2, KEYS, ROWS), F32),
            pltpu.VMEM((4, 8, ROWS), F32),
            pltpu.VMEM((ROWS, SLAB), BF16),
            pltpu.VMEM((ROWS, SLAB), F32),
            pltpu.VMEM((2, KEYS, SLAB), F32),
            pltpu.VMEM((2, KEYS, SLAB), F32),
            pltpu.VMEM((2, KEYS, SLAB), BF16),
            pltpu.VMEM((2, KEYS, SLAB), BF16),
            pltpu.VMEM((2, KEYS, SLAB), BF16),
            pltpu.VMEM((4, ROWS, HEAD), BF16),
            pltpu.SemaphoreType.DMA((N_MOVES,)),
            pltpu.SemaphoreType.DMA((N_MOVES,)),
            pltpu.SemaphoreType.DMA((5,)),
            pltpu.SemaphoreType.DMA((2,)),
            pltpu.SemaphoreType.DMA((3,)),
        ],
        compiler_params=pltpu.CompilerParams(
            collective_id=0, has_side_effects=True, vmem_limit_bytes=54 * 1024 * 1024
        ),
    )(boundary_grad, w_out, context, queries, keys, values)
    return pl.pallas_call(
        write_out,
        out_shape=[jax.ShapeDtypeStruct(shape, BF16) for shape in shapes],
        in_specs=[vmem_spec] * 4,
        out_specs=[any_spec] * 4,
        scratch_shapes=[pltpu.SemaphoreType.DMA((9,))],
    )(*grads)


def solution(mesh):
    in_specs = (
        P("section", "col", "row"),
        P("section", "col", "row"),
        P("section", "row", "col"),
        P("section", "row", "col"),
        P("section", "row", "col"),
        P("section", "row", "col"),
    )
    out_specs = (
        P("section", "col", "row"),
        P("section", "row", "col"),
        P("section", "row", "col"),
        P("section", "row", "col"),
    )
    return jax.shard_map(local, mesh=mesh, in_specs=in_specs, out_specs=out_specs, check_vma=False)
```

time: 410 us -> 102 us (0.25)
  waiting for transfers between devices: 329 us -> 0 us
  Pallas kernels: 0 us -> 97 us
  matrix products: 36.3 us -> 0 us
  between operations: 14.3 us -> 0.83 us
  local copies, waits for them, and re-layouts: 17.6 us -> 4.41 us
  other arithmetic: 6.31 us -> 0 us
  starting transfers between devices: 5.75 us -> 0 us
    all_gather x4 -> x0, waiting for transfers between devices: 204 us -> none  [the longest x1 132 us: local(): grad_rows = lax.all_gather(arriving, 'col', axis=0, tiled=True)]
    reduce_scatter x3 -> x0, waiting for transfers between devices: 104 us -> none  [the longest x1 41.2 us: local(): lax.psum_scatter(partial_v, 'row', scatter_dimension=0, tiled=True)]
    pallas_call x0 -> x2, Pallas kernels: none -> 97 us  [the longest x1 91.7 us: local(): pl.pallas_call(kernel, out_shape=[pltpu.VMEM(shape, BF16) for shape in sh...]
    dot_general x6 -> x0, matrix products: 29.8 us -> none  [the longest x1 9.73 us: local(): lax.dot_general(block, weight, (((1,), (1,)), ((), ())), preferred_elemen...]
    ppermute x1 -> x0, waiting for transfers between devices: 19.4 us -> none  [shifted(): return lax.ppermute(block, axis, route)]
    unnamed x22 -> x8, local copies, waits for them, and re-layouts: 12.7 us -> 4.41 us
    sub x1 -> x0, matrix products: 6.44 us -> none  [attend_backward(): weights = jnp.exp(scores - top)]
    ppermute x1 -> x0, starting transfers between devices: 5.28 us -> none  [shifted(): return lax.ppermute(block, axis, route)]
  transfers between devices with their start and end apart: 8 -> 0, of which waited for: 8 -> 0; matrix products, arithmetic and copies ran while one was open for 13% -> 0% of each run, Pallas kernels for 0% -> 0%
where the time goes in v1:
time: 102 us
  Pallas kernels  97 us (95%)
  local copies, waits for them, and re-layouts  4.41 us (4%)
    pallas_call x1, Pallas kernels, local(): pl.pallas_call(kernel, out_shape=[pltpu.VMEM(shape, BF16) for shape in sh...  91.7 us
    pallas_call x1, Pallas kernels, local(): pl.pallas_call(write_out, out_shape=[jax.ShapeDtypeStruct(shape, BF16) fo...  5.25 us
    unnamed x8, local copies, waits for them, and re-layouts  4.41 us

profile of v1, /device:TPU:1, one launch (start us, length us, event | category | flops | bytes accessed | tf_op | source)
XLA Modules:
  0.0 102.2 jit_solution(2428066316030485159)
XLA Ops:
  0.6 91.7 %shard_map.93 = (bf16[1,768,3072]{2,1,0:T(8,128)(2,1)S(1)}, bf16[1,256,768]{2,1,0:T(8,128)(2,1)S(1)}, bf16[1,256,768]{2,1,0:T(8,128)(2,1)S(1)}, bf16[1,256,768]{2,1,0:T(8,128)(2,1)S(1)}) custom-call(bf16[1,128,3072]{2,1,0:T(8,128)(2,1)} %bg.1, bf16[1,768,3072]{2,1,0:T(8,128)(2,1)} %wo.1, bf16[1,256,768]{2,1,0:T(8,128)(2,1)} %cx.1, bf16[1,256,768]{2,1,0:T(8,128)(2,1)} %qs.1, ...), custom_call_target="tpu_custom_call" | custom-call | tf_op jit(solution)/shard_map/pallas_call | solution.py:436
  92.4 0.0 copy-start
  92.4 2.1 %copy-done = bf16[1,768,3072]{2,1,0:T(8,128)(2,1)} copy-done((bf16[1,768,3072]{2,1,0:T(8,128)(2,1)}, bf16[1,768,3072]{2,1,0:T(8,128)(2,1)S(1)}, u32[]{:S(2)}) %copy-start) | copy-done | bytes 4718616
  94.5 0.0 copy-start.1
  94.5 0.8 copy-done.1
  95.3 0.0 copy-start.2
  95.3 0.8 copy-done.2
  96.0 0.0 copy-start.3
  96.0 0.8 copy-done.3
  96.8 5.2 %shard_map.94 = (bf16[1,768,3072]{2,1,0:T(8,128)(2,1)}, bf16[1,256,768]{2,1,0:T(8,128)(2,1)}, bf16[1,256,768]{2,1,0:T(8,128)(2,1)}, bf16[1,256,768]{2,1,0:T(8,128)(2,1)}) custom-call(bf16[1,768,3072]{2,1,0:T(8,128)(2,1)} %copy-done, bf16[1,256,768]{2,1,0:T(8,128)(2,1)} %copy-done.1, bf16[1,256,768]{2,1,0:T(8,128)(2,1)} %copy-done.2, ...), custom_call_target="tpu_custom_call" | custom-call | tf_op jit(solution)/shard_map/pallas_call | solution.py:476
Async XLA Ops:
  92.4 2.1 %copy-start = (bf16[1,768,3072]{2,1,0:T(8,128)(2,1)}, bf16[1,768,3072]{2,1,0:T(8,128)(2,1)S(1)}, u32[]{:S(2)}) copy-start(bf16[1,768,3072]{2,1,0:T(8,128)(2,1)S(1)} %get-tuple-element.8.gw) | copy-start | bytes 14155780
  94.5 0.8 copy-start.1
  95.3 0.8 copy-start.2
  96.0 0.8 copy-start.3

commit v2 on v1

--- a/solution.py
+++ b/solution.py
@@ -22,16 +22,16 @@
 TILE = 512
 
 ORDER0 = [
-    "E1", "E0", "e0l", "q", "e0r", "k", "e1l", "cB", "e1r", "cA", "kf", "f0", "f1", "qf", "cfB", "zs1", "P0", "P1",
-    "cfA", "zs0", "t0", "p0", "g0a", "zr1", "t1", "zr1r", "P2", "v", "zr0l", "t2", "s0", "g0b", "f3", "vf", "zr0",
-    "p1", "f2", "t3", "P3", "a0", "s1", "p2", "g1a", "p3", "g1b", "s2", "a1", "g2a", "g2b", "dq", "s3", "a2", "g3a",
-    "dqf", "g3b", "a3", "dk", "dv", "dql",
+    "E0", "cA", "e1l", "e0r", "k", "f1", "q", "E1", "cB", "f0", "kf", "zs1", "e0l", "e1r", "qf", "v", "cfA", "cfB",
+    "p0", "zr1r", "zs0", "t0", "g0a", "vf", "f3", "s0", "zr1", "P0", "t1", "p1", "zr0l", "a0", "P1", "zr0", "f2",
+    "t2", "g0b", "t3", "s1", "g1a", "P2", "a1", "P3", "dq", "p2", "p3", "dqf", "g1b", "g2a", "s2", "s3", "a2",
+    "g2b", "g3a", "a3", "g3b", "dk", "dv", "dql",
 ]
 ORDER1 = [
-    "E1", "q", "cB", "E0", "e0l", "e0r", "k", "cA", "e1l", "e1r", "kf", "f0", "f1", "qf", "zs1", "P0", "cfB", "P1",
-    "cfA", "zs0", "t0", "p0", "zr1r", "g0a", "zr1", "t1", "v", "P2", "zr0l", "s0", "g0b", "f3", "zr0", "p1", "t2",
-    "f2", "vf", "P3", "a0", "s1", "p2", "g1a", "p3", "g1b", "s2", "t3", "a1", "g2a", "g2b", "dq", "s3", "a2", "g3a",
-    "dqf", "g3b", "a3", "dk", "dv", "dql",
+    "cB", "E1", "cA", "E0", "k", "kf", "e0l", "e0r", "q", "qf", "f0", "zs1", "cfA", "e1l", "cfB", "e1r", "P0", "P1",
+    "f1", "v", "t0", "zs0", "t1", "p0", "zr1", "f3", "s0", "vf", "g0a", "t2", "zr1r", "p1", "zr0l", "g0b", "zr0",
+    "s1", "a0", "P2", "f2", "g1a", "a1", "g1b", "dq", "p2", "p3", "t3", "P3", "s2", "g2a", "s3", "dqf", "g2b", "a2",
+    "a3", "g3a", "g3b", "dk", "dv", "dql",
 ]
 
 
@@ -476,9 +476,10 @@
     return pl.pallas_call(
         write_out,
         out_shape=[jax.ShapeDtypeStruct(shape, BF16) for shape in shapes],
-        in_specs=[vmem_spec] * 4,
+        in_specs=[any_spec] * 4,
         out_specs=[any_spec] * 4,
         scratch_shapes=[pltpu.SemaphoreType.DMA((9,))],
+        compiler_params=pltpu.CompilerParams(vmem_limit_bytes=1024 * 1024),
     )(*grads)
 
 

time: 102 us -> 96.1 us (0.942); the launches traced: 102 us -> 95.1 us
  local copies, waits for them, and re-layouts: 4.41 us -> 0 us
  Pallas kernels: 97 us -> 94.3 us
    unnamed x8 -> x0, local copies, waits for them, and re-layouts: 4.41 us -> none
    pallas_call x1, Pallas kernels: 5.25 us -> 2.62 us  [local(): pl.pallas_call(write_out, out_shape=[jax.ShapeDtypeStruct(shape, BF16) fo...]
where the time goes in v2:
time: 96.1 us; the launch traced here: 95.1 us
  Pallas kernels  94.3 us (98%)
    pallas_call x1, Pallas kernels, local(): pl.pallas_call(kernel, out_shape=[pltpu.VMEM(shape, BF16) for shape in sh...  91.6 us
    pallas_call x1, Pallas kernels, local(): pl.pallas_call(write_out, out_shape=[jax.ShapeDtypeStruct(shape, BF16) fo...  2.62 us

profile of v2, /device:TPU:1, one launch (start us, length us, event | category | flops | bytes accessed | tf_op | source)
XLA Modules:
  0.0 95.1 jit_solution(2442545831055602568)
XLA Ops:
  0.6 91.6 %shard_map.93 = (bf16[1,768,3072]{2,1,0:T(8,128)(2,1)S(1)}, bf16[1,256,768]{2,1,0:T(8,128)(2,1)S(1)}, bf16[1,256,768]{2,1,0:T(8,128)(2,1)S(1)}, bf16[1,256,768]{2,1,0:T(8,128)(2,1)S(1)}) custom-call(bf16[1,128,3072]{2,1,0:T(8,128)(2,1)} %bg.1, bf16[1,768,3072]{2,1,0:T(8,128)(2,1)} %wo.1, bf16[1,256,768]{2,1,0:T(8,128)(2,1)} %cx.1, bf16[1,256,768]{2,1,0:T(8,128)(2,1)} %qs.1, ...), custom_call_target="tpu_custom_call" | custom-call | tf_op jit(solution)/shard_map/pallas_call | solution.py:436
  92.3 2.6 %shard_map.94 = (bf16[1,768,3072]{2,1,0:T(8,128)(2,1)}, bf16[1,256,768]{2,1,0:T(8,128)(2,1)}, bf16[1,256,768]{2,1,0:T(8,128)(2,1)}, bf16[1,256,768]{2,1,0:T(8,128)(2,1)}) custom-call(bf16[1,768,3072]{2,1,0:T(8,128)(2,1)S(1)} %get-tuple-element.8.gw, bf16[1,256,768]{2,1,0:T(8,128)(2,1)S(1)} %get-tuple-element.9.gq, ...), custom_call_target="tpu_custom_call" | custom-call | tf_op jit(solution)/shard_map/pallas_call | solution.py:476

commit v3 on v2

--- a/solution.py
+++ b/solution.py
@@ -13,7 +13,9 @@
 
 ROWS = 256
 PIECE = 128
-HALF = 64
+CHUNKS = 2
+CHUNK = PIECE // CHUNKS
+LOW = 192
 KEYS = 512
 FEAT = 3072
 WIDTH = 768
@@ -22,16 +24,14 @@
 TILE = 512
 
 ORDER0 = [
-    "E0", "cA", "e1l", "e0r", "k", "f1", "q", "E1", "cB", "f0", "kf", "zs1", "e0l", "e1r", "qf", "v", "cfA", "cfB",
-    "p0", "zr1r", "zs0", "t0", "g0a", "vf", "f3", "s0", "zr1", "P0", "t1", "p1", "zr0l", "a0", "P1", "zr0", "f2",
-    "t2", "g0b", "t3", "s1", "g1a", "P2", "a1", "P3", "dq", "p2", "p3", "dqf", "g1b", "g2a", "s2", "s3", "a2",
-    "g2b", "g3a", "a3", "g3b", "dk", "dv", "dql",
+    "E0", "l0", "r0", "q", "cA", "l1", "f0", "E1", "qf", "k", "f1", "cB", "r1", "z1", "kf", "F0", "R1", "z0", "cfB",
+    "L1", "p0", "cfA", "v", "p1", "R0", "L0", "P0", "s0", "t0", "P1", "t1", "F1", "t2", "P2", "vf", "gA", "s1",
+    "p2", "gB", "a0", "p3", "s2", "a1", "t3", "dq", "s3", "a2", "gC", "P3", "a3", "gD", "dqf", "dk", "dv", "dql",
 ]
 ORDER1 = [
-    "cB", "E1", "cA", "E0", "k", "kf", "e0l", "e0r", "q", "qf", "f0", "zs1", "cfA", "e1l", "cfB", "e1r", "P0", "P1",
-    "f1", "v", "t0", "zs0", "t1", "p0", "zr1", "f3", "s0", "vf", "g0a", "t2", "zr1r", "p1", "zr0l", "g0b", "zr0",
-    "s1", "a0", "P2", "f2", "g1a", "a1", "g1b", "dq", "p2", "p3", "t3", "P3", "s2", "g2a", "s3", "dqf", "g2b", "a2",
-    "a3", "g3a", "g3b", "dk", "dv", "dql",
+    "E0", "cB", "k", "q", "cA", "E1", "cfB", "qf", "v", "l0", "r0", "f0", "cfA", "kf", "l1", "r1", "t0", "f1", "t1",
+    "z1", "P0", "vf", "P1", "p0", "t2", "L1", "z0", "P2", "s0", "R1", "F0", "p1", "gA", "R0", "L0", "t3", "gB",
+    "s1", "F1", "P3", "a0", "a1", "dq", "p2", "p3", "s2", "gC", "dqf", "s3", "gD", "a2", "a3", "dk", "dv", "dql",
 ]
 
 
@@ -42,7 +42,7 @@
 def kernel(
     bg, wo, cx, qs, ks, vs,
     gw, gq, gk, gv,
-    inc, wv, ctx, ctxt, acc, q2, k2, v2, qg, part, partb, got_a, got_b, sumb, pt, linv, dout,
+    inc, wv, ctx, ctxt, acc, q2, k2, v2, qg, part, partb, got_a, got_b, sumb, kt, pt, linv, dout,
     dqa, dka, dva, dqb, dkb, dvb, stage,
     send, recv, lsem, esem, osem,
 ):
@@ -105,28 +105,30 @@
     in_pair_b = pl.ds(m128(HEAD * par_b), SLAB)
     own_full = pl.ds(m128(HEAD * par), HEAD)
 
-    def slot(yy, zz, h):
-        half = yy // 2
-        return inc.at[2 * zz + half, pl.ds(pl.multiple_of(PIECE * (yy - 2 * half) + HALF * h, HALF), HALF)]
-
-    groups = [2 * z + y // 2, 2 * z + 1 - y // 2, 2 * zp + y // 2, 2 * zp + 1 - y // 2]
+    def slot(yy, zz, q):
+        return inc.at[zz, pl.ds(pl.multiple_of(PIECE * yy + CHUNK * q, CHUNK), CHUNK)]
+
+    groups = [(z, y // 2), (z, 1 - y // 2), (zp, y // 2), (zp, 1 - y // 2)]
 
     moves = {}
 
     def move(tag, src, there, here, dev):
         moves[tag] = (len(moves), src, there, here, dev)
 
-    for h in range(2):
-        move("E%d" % h, bg.at[0, pl.ds(HALF * h, HALF)], slot(y, z, h), slot(y, z, h), dev_prev)
-        move("z%d" % h, slot(y, z, h), slot(y, z, h), slot(y, zp, h), dev_z)
-        move("l_own%d" % h, slot(y, z, h), slot(y, z, h), slot(y_l, z, h), dev_r)
-        move("r_own%d" % h, slot(y, z, h), slot(y, z, h), slot(y_r, z, h), dev_l)
-        move("l_oth%d" % h, slot(y, zp, h), slot(y, zp, h), slot(y_l, zp, h), dev_r)
-        move("r_oth%d" % h, slot(y, zp, h), slot(y, zp, h), slot(y_r, zp, h), dev_l)
-    move("o_own0", slot(y_l, z, 0), slot(y_l, z, 0), slot(y_o, z, 0), dev_r)
-    move("o_own1", slot(y_r, z, 1), slot(y_r, z, 1), slot(y_o, z, 1), dev_l)
-    move("o_oth1", slot(y_r, zp, 1), slot(y_r, zp, 1), slot(y_o, zp, 1), dev_l)
-    move("o_oth0", slot(y_o, z, 0), slot(y_o, z, 0), slot(y_o, zp, 0), dev_z)
+    for q in range(CHUNKS):
+        move("E%d" % q, bg.at[0, pl.ds(CHUNK * q, CHUNK)], slot(y, z, q), slot(y, z, q), dev_prev)
+        move("z%d" % q, slot(y, z, q), slot(y, z, q), slot(y, zp, q), dev_z)
+        move("l_own%d" % q, slot(y, z, q), slot(y, z, q), slot(y_l, z, q), dev_r)
+        move("r_own%d" % q, slot(y, z, q), slot(y, z, q), slot(y_r, z, q), dev_l)
+        move("l_oth%d" % q, slot(y, zp, q), slot(y, zp, q), slot(y_l, zp, q), dev_r)
+        move("r_oth%d" % q, slot(y, zp, q), slot(y, zp, q), slot(y_r, zp, q), dev_l)
+        if q < CHUNKS // 2:
+            move("o_own%d" % q, slot(y_l, z, q), slot(y_l, z, q), slot(y_o, z, q), dev_r)
+            move("o_oth%d" % q, slot(y_o, z, q), slot(y_o, z, q), slot(y_o, zp, q), dev_z)
+        else:
+            move("o_own%d" % q, slot(y_r, z, q), slot(y_r, z, q), slot(y_o, z, q), dev_l)
+            move("o_oth%d" % q, slot(y_r, zp, q), slot(y_r, zp, q), slot(y_o, zp, q), dev_l)
+
     def block(xx, start=0, size=ROWS):
         half = xx // 2
         return half, pl.ds(m128(ROWS * (xx - 2 * half) + start), size)
@@ -138,11 +140,11 @@
         move(n + "C", b.at[(*from_a, in_pair_b)], b.at[(*from_a, in_pair_b)], b.at[(*from_c, in_pair)], dev_b)
     move("cA", cx.at[0], ctx.at[x], ctx.at[x_a], dev_a)
     move("cB", cx.at[0], ctx.at[x], ctx.at[x_b], dev_b)
-    lo, hi = pl.ds(0, ROWS // 2), pl.ds(ROWS // 2, ROWS // 2)
+    lo, hi = pl.ds(0, LOW), pl.ds(LOW, ROWS - LOW)
     move("cC0", ctx.at[x_a, lo], ctx.at[x_a, lo], ctx.at[x_c, lo], dev_b)
     move("cC1", ctx.at[x_b, hi], ctx.at[x_b, hi], ctx.at[x_c, hi], dev_a)
     for k in range(4):
-        move("rsA%d" % k, partb.at[k, :, pair_of(x_a)], got_a.at[k], got_a.at[k], dev_a)
+        move("rsA%d" % k, partb.at[k, pair_of(x_a)], got_a.at[k], got_a.at[k], dev_a)
         move("rsB%d" % k, sumb.at[k], got_b.at[k], got_b.at[k], dev_b)
 
     def move_out(n, src, dst, start, size, where):
@@ -167,8 +169,8 @@
         i, _, _, here, dev = moves[tag]
         return pltpu.make_async_remote_copy(here, here, send.at[i], recv.at[i], device_id=dev, device_id_type=MESH)
 
-    def entry_kept(h):
-        return pltpu.make_async_copy(bg.at[0, pl.ds(HALF * h, HALF)], slot(y, z, h), esem.at[h])
+    def entry_kept(q):
+        return pltpu.make_async_copy(bg.at[0, pl.ds(CHUNK * q, CHUNK)], slot(y, z, q), esem.at[q])
 
     loads = []
     for src, dst in (
@@ -211,21 +213,18 @@
             arriving(tag).wait_recv()
 
     def group_rows(g):
-        zz = g // 2
-        return g - 2 * zz, zz, pl.ds(m128(PIECE * zz), PIECE), pl.ds(m128(ROWS + PIECE * zz), PIECE)
+        zz, p = g
+        return p, zz, pl.ds(m128(PIECE * zz), PIECE), pl.ds(m128(ROWS + PIECE * zz), PIECE)
 
     def partial_grad(k):
-        g = groups[k]
-
-        @pl.loop(0, 3)
-        def _(n):
-            rows = pl.ds(pl.multiple_of(n * 256, 256), 256)
-            r = dot(inc[g], wv[rows], 1, 1)
-            part[k, :, rows] = r
-            partb[k, :, rows] = r.astype(BF16)
+        zz, p = groups[k]
+        tokens = pl.ds(pl.multiple_of(ROWS * p, ROWS), ROWS)
+        r = dot(wv[...], inc[zz, tokens], 1, 1)
+        part[k] = r
+        partb[k] = r.astype(BF16)
 
     def pass_on(k):
-        r = part[k, :, slab_of(x_b)] + got_a[k, :, in_pair_b].astype(F32)
+        r = part[k, slab_of(x_b)] + got_a[k, in_pair_b].astype(F32)
         sumb[k] = r.astype(BF16)
 
     heads = [pl.ds(HEAD * h, HEAD) for h in range(2)]
@@ -236,6 +235,10 @@
         row = lax.broadcasted_iota(jnp.int32, (KEYS, ROWS), 0)
         lane = lax.broadcasted_iota(jnp.int32, (KEYS, ROWS), 1)
         ahead = jnp.where(lane < PIECE, lane, lane + PIECE) - row
+        if k == 0:
+            for j in range(2):
+                for h in range(2):
+                    kt[j, heads[h]] = k2[j, :, pheads[h]].T
         for h in range(2):
             qg[k, 0:PIECE, heads[h]] = q2[p, rows0, pheads[h]]
             qg[k, PIECE:ROWS, heads[h]] = q2[p, rows1, pheads[h]]
@@ -268,58 +271,49 @@
 
     def turn(k):
         p, _, rows, _ = group_rows(groups[k])
-        ctxt[k, :, 0:PIECE] = ctx[2 * p, rows].T
-        ctxt[k, :, PIECE:ROWS] = ctx[2 * p + 1, rows].T
-
-    def weight_grad(k, half, first):
-        g = groups[k]
+        ctxt[k // 2, :, pl.ds(m128(ROWS * p), PIECE)] = ctx[2 * p, rows].T
+        ctxt[k // 2, :, pl.ds(m128(ROWS * p + PIECE), PIECE)] = ctx[2 * p + 1, rows].T
+
+    def weight_grad(i, half):
+        zz = (z, zp)[i]
 
         @pl.loop(0, FEAT // TILE // 2)
         def _(n):
             cols = pl.ds(pl.multiple_of(half * (FEAT // 2) + n * TILE, TILE), TILE)
-            r = dot(ctxt[k], inc[g, :, cols], 1, 0)
-            if not first:
-                r = r + acc[:, cols]
-            if k == 3:
-                gw[0, :, cols] = r.astype(BF16)
+            r = dot(ctxt[i], inc[zz, :, cols], 1, 0)
+            if i == 0:
+                acc[:, cols] = r
             else:
-                acc[:, cols] = r
+                gw[0, :, cols] = (r + acc[:, cols]).astype(BF16)
 
     def attend(k):
         p, _, rows0, rows1 = group_rows(groups[k])
         if k == 0:
             dka[...] = jnp.zeros_like(dka)
             dva[...] = jnp.zeros_like(dva)
-        grad = part[k, :, own_slab] + got_a[k, :, in_pair].astype(F32) + got_b[k].astype(F32)
+        grad = part[k, own_slab] + got_a[k, in_pair].astype(F32) + got_b[k].astype(F32)
         gb = grad.astype(BF16)
         dout[...] = gb
-        rounded = gb.astype(F32)
-        top = (rounded[0:PIECE] * ctx[2 * p, rows0, own_slab].astype(F32)).T
-        low = (rounded[PIECE:ROWS] * ctx[2 * p + 1, rows0, own_slab].astype(F32)).T
-        deltas = []
-        for h in range(2):
-            sel = slice(HEAD * h, HEAD * (h + 1))
-            deltas.append(
-                jnp.concatenate(
-                    [jnp.sum(top[sel], axis=0, keepdims=True), jnp.sum(low[sel], axis=0, keepdims=True)], axis=1
-                )
-            )
+        tokens = pl.ds(pl.multiple_of(ROWS * p, ROWS), ROWS)
+        prod = gb.astype(F32) * ctxt[k // 2, own_slab, tokens].astype(F32)
+        deltas = [jnp.sum(prod[HEAD * h : HEAD * (h + 1)], axis=0, keepdims=True) for h in range(2)]
         inv = [linv[k, h : h + 1] for h in range(2)]
         dqa[...] = jnp.zeros_like(dqa)
 
         @pl.loop(0, p + 1)
         def _(j):
             for h in range(2):
-                gh = dout[:, heads[h]]
+                gh = dout[heads[h]]
                 w = pt[h, k, j] * inv[h]
-                dp = dot(v2[j, :, pheads[h]], gh, 1, 1)
+                dp = dot(v2[j, :, pheads[h]], gh, 1, 0)
                 ds = (w * (dp - deltas[h])).astype(BF16)
-                dva[j, :, heads[h]] += dot(w.astype(BF16), gh, 1, 0)
+                dva[j, :, heads[h]] += dot(w.astype(BF16), gh, 1, 1)
                 dka[j, :, heads[h]] += dot(ds, qg[k, :, heads[h]], 1, 0)
-                dqa[:, heads[h]] += dot(ds, k2[j, :, pheads[h]], 0, 0)
-
-        dqb[p, rows0] = (dqa[0:PIECE] * SCALE).astype(BF16)
-        dqb[p, rows1] = (dqa[PIECE:ROWS] * SCALE).astype(BF16)
+                dqa[heads[h]] += dot(kt[j, heads[h]], ds, 1, 0)
+
+        dq = (dqa[...] * SCALE).astype(BF16).T
+        dqb[p, rows0] = dq[0:PIECE]
+        dqb[p, rows1] = dq[PIECE:ROWS]
 
     def cast_keys():
         dkb[...] = (dka[...] * SCALE).astype(BF16)
@@ -328,40 +322,40 @@
         dvb[...] = dva[...].astype(BF16)
 
     table = {
-        "E0": ([], None, ["E0"]),
-        "E1": ([], None, ["E1"]),
         "cA": ([], None, ["cA"]),
         "cB": ([], None, ["cB"]),
         "cfA": (["cA"], None, ["cC0"]),
         "cfB": (["cB"], None, ["cC1"]),
-        "e0r": (["E0"], None, ["l_own0"]),
-        "e0l": (["E0"], None, ["r_own0"]),
-        "e1l": (["E1"], None, ["r_own1"]),
-        "e1r": (["E1"], None, ["l_own1"]),
-        "zs0": (["E0"], None, ["z0"]),
-        "zs1": (["E1"], None, ["z1"]),
-        "f0": (["l_own0"], None, ["o_own0"]),
-        "f1": (["r_own1"], None, ["o_own1"]),
-        "f2": (["r_oth1"], None, ["o_oth1"]),
-        "f3": (["o_own0"], None, ["o_oth0"]),
-        "zr0": (["z0"], None, ["l_oth0"]),
-        "zr0l": (["z0"], None, ["r_oth0"]),
-        "zr1": (["z1"], None, ["r_oth1"]),
-        "zr1r": (["z1"], None, ["l_oth1"]),
         "dq": ([], None, ["dqe1", "dqeA", "dqeB"]),
         "dqf": (["dqe1"], None, ["dqeC"]),
         "dk": ([], cast_keys, ["dk1", "dkA", "dkB"]),
         "dv": ([], cast_values, ["dv1", "dvA", "dvB"]),
         "dql": ([], None, ["dql1", "dqlA", "dqlB"]),
+        "gA": ([], lambda: weight_grad(0, 0), []),
+        "gB": ([], lambda: weight_grad(0, 1), []),
+        "gC": ([], lambda: weight_grad(1, 0), []),
+        "gD": ([], lambda: weight_grad(1, 1), []),
     }
-    own = ["E0", "E1"]
-    near = ["l_own0", "l_own1", "r_own0", "r_own1"]
-    far = ["o_own0", "o_own1"]
-    near_z = ["z0", "z1", "l_oth0", "l_oth1", "r_oth0", "r_oth1"]
-    far_z = ["o_oth0", "o_oth1"]
     for n in "kqv":
         table[n] = ([], None, [n + "A", n + "B"])
         table[n + "f"] = ([n + "A"], None, [n + "C"])
+    own, near, far, near_z, far_z = [], [], [], [], []
+    for q in range(CHUNKS):
+        i = str(q)
+        first = q < CHUNKS // 2
+        table["E" + i] = ([], None, ["E" + i])
+        table["r" + i] = (["E" + i], None, ["l_own" + i])
+        table["l" + i] = (["E" + i], None, ["r_own" + i])
+        table["z" + i] = (["E" + i], None, ["z" + i])
+        table["R" + i] = (["z" + i], None, ["l_oth" + i])
+        table["L" + i] = (["z" + i], None, ["r_oth" + i])
+        table["f" + i] = (["l_own" + i] if first else ["r_own" + i], None, ["o_own" + i])
+        table["F" + i] = (["o_own" + i] if first else ["r_oth" + i], None, ["o_oth" + i])
+        own += ["E" + i]
+        near += ["l_own" + i, "r_own" + i]
+        far += ["o_own" + i]
+        near_z += ["z" + i, "l_oth" + i, "r_oth" + i]
+        far_z += ["o_oth" + i]
     for k, need in enumerate((["@4"] + own + near, far, near_z, far_z)):
         table["p%d" % k] = (need, lambda k=k: partial_grad(k), ["rsA%d" % k])
         table["s%d" % k] = (["rsA%d" % k], lambda k=k: pass_on(k), ["rsB%d" % k])
@@ -371,13 +365,7 @@
 
     def perform(order):
         seen = set()
-        touched = set()
         for name in order:
-            if name[0] == "g":
-                k, half = int(name[1]), "ab".index(name[2])
-                weight_grad(k, half, half not in touched)
-                touched.add(half)
-                continue
             waits, work, sends = table[name]
             for tag in waits:
                 if tag not in seen:
@@ -413,7 +401,7 @@
             outgoing(tag).wait_send()
 
 
-N_MOVES = 2 * 6 + 4 + 9 + 4 + 8 + 16
+N_MOVES = 8 * CHUNKS + 9 + 4 + 8 + 16
 
 
 def write_out(gw, gq, gk, gv, gw_out, gq_out, gk_out, gv_out, sems):
@@ -439,20 +427,21 @@
         in_specs=[any_spec] * 6,
         out_specs=[vmem_spec] * 4,
         scratch_shapes=[
-            pltpu.VMEM((4, ROWS, FEAT), BF16),
+            pltpu.VMEM((2, KEYS, FEAT), BF16),
             pltpu.VMEM((WIDTH, FEAT), BF16),
             pltpu.VMEM((4, ROWS, WIDTH), BF16),
-            pltpu.VMEM((4, WIDTH, ROWS), BF16),
+            pltpu.VMEM((2, WIDTH, KEYS), BF16),
             pltpu.VMEM((WIDTH, FEAT), F32),
             pltpu.VMEM((2, KEYS, PAIR), BF16),
             pltpu.VMEM((2, KEYS, PAIR), BF16),
             pltpu.VMEM((2, KEYS, PAIR), BF16),
             pltpu.VMEM((4, ROWS, SLAB), BF16),
-            pltpu.VMEM((4, ROWS, WIDTH), F32),
-            pltpu.VMEM((4, ROWS, WIDTH), BF16),
-            pltpu.VMEM((4, ROWS, PAIR), BF16),
-            pltpu.VMEM((4, ROWS, SLAB), BF16),
-            pltpu.VMEM((4, ROWS, SLAB), BF16),
+            pltpu.VMEM((4, WIDTH, ROWS), F32),
+            pltpu.VMEM((4, WIDTH, ROWS), BF16),
+            pltpu.VMEM((4, PAIR, ROWS), BF16),
+            pltpu.VMEM((4, SLAB, ROWS), BF16),
+            pltpu.VMEM((4, SLAB, ROWS), BF16),
+            pltpu.VMEM((2, SLAB, KEYS), BF16),
             pltpu.VMEM((2, 4, 2, KEYS, ROWS), F32),
             pltpu.VMEM((4, 8, ROWS), F32),
             pltpu.VMEM((ROWS, SLAB), BF16),
@@ -466,7 +455,7 @@
             pltpu.SemaphoreType.DMA((N_MOVES,)),
             pltpu.SemaphoreType.DMA((N_MOVES,)),
             pltpu.SemaphoreType.DMA((5,)),
-            pltpu.SemaphoreType.DMA((2,)),
+            pltpu.SemaphoreType.DMA((CHUNKS,)),
             pltpu.SemaphoreType.DMA((3,)),
         ],
         compiler_params=pltpu.CompilerParams(

time: 96.1 us -> 92.2 us (0.959)
  Pallas kernels: 94.3 us -> 91.3 us
    pallas_call x1, Pallas kernels: 91.6 us -> 88.7 us  [local(): pl.pallas_call(kernel, out_shape=[pltpu.VMEM(shape, BF16) for shape in sh...]
where the time goes in v3:
time: 92.2 us; the launch traced here: 92.1 us
  Pallas kernels  91.3 us (99%)
    pallas_call x1, Pallas kernels, local(): pl.pallas_call(kernel, out_shape=[pltpu.VMEM(shape, BF16) for shape in sh...  88.7 us
    pallas_call x1, Pallas kernels, local(): pl.pallas_call(write_out, out_shape=[jax.ShapeDtypeStruct(shape, BF16) fo...  2.62 us

profile of v3, /device:TPU:1, one launch (start us, length us, event | category | flops | bytes accessed | tf_op | source)
XLA Modules:
  0.0 92.1 jit_solution(16225456484596498565)
XLA Ops:
  0.6 88.7 %shard_map.93 = (bf16[1,768,3072]{2,1,0:T(8,128)(2,1)S(1)}, bf16[1,256,768]{2,1,0:T(8,128)(2,1)S(1)}, bf16[1,256,768]{2,1,0:T(8,128)(2,1)S(1)}, bf16[1,256,768]{2,1,0:T(8,128)(2,1)S(1)}) custom-call(bf16[1,128,3072]{2,1,0:T(8,128)(2,1)} %bg.1, bf16[1,768,3072]{2,1,0:T(8,128)(2,1)} %wo.1, bf16[1,256,768]{2,1,0:T(8,128)(2,1)} %cx.1, bf16[1,256,768]{2,1,0:T(8,128)(2,1)} %qs.1, ...), custom_call_target="tpu_custom_call" | custom-call | tf_op jit(solution)/shard_map/pallas_call | solution.py:424
  89.3 2.6 %shard_map.94 = (bf16[1,768,3072]{2,1,0:T(8,128)(2,1)}, bf16[1,256,768]{2,1,0:T(8,128)(2,1)}, bf16[1,256,768]{2,1,0:T(8,128)(2,1)}, bf16[1,256,768]{2,1,0:T(8,128)(2,1)}) custom-call(bf16[1,768,3072]{2,1,0:T(8,128)(2,1)S(1)} %get-tuple-element.8.gw, bf16[1,256,768]{2,1,0:T(8,128)(2,1)S(1)} %get-tuple-element.9.gq, ...), custom_call_target="tpu_custom_call" | custom-call | tf_op jit(solution)/shard_map/pallas_call | solution.py:465

commit v4 on v3

--- a/solution.py
+++ b/solution.py
@@ -24,14 +24,16 @@
 TILE = 512
 
 ORDER0 = [
-    "E0", "l0", "r0", "q", "cA", "l1", "f0", "E1", "qf", "k", "f1", "cB", "r1", "z1", "kf", "F0", "R1", "z0", "cfB",
-    "L1", "p0", "cfA", "v", "p1", "R0", "L0", "P0", "s0", "t0", "P1", "t1", "F1", "t2", "P2", "vf", "gA", "s1",
-    "p2", "gB", "a0", "p3", "s2", "a1", "t3", "dq", "s3", "a2", "gC", "P3", "a3", "gD", "dqf", "dk", "dv", "dql",
+    "E1", "q", "r0", "k", "l0", "l1", "f0", "cB", "E0", "kf", "cA", "r1", "cfA", "f1", "z1", "cfB", "v", "z0", "p0",
+    "F0", "R1", "L1", "p1", "L0", "t0", "R0", "qf", "s0", "t1", "vf", "t2", "gA", "F1", "P0", "a0", "P1", "p2",
+    "s1", "P2", "p3", "gB", "s2", "P3", "a1", "dq", "s3", "a2", "dqf", "t3", "gC", "a3", "dql", "gD", "dk", "dqlf",
+    "dkf", "dv", "dvf",
 ]
 ORDER1 = [
-    "E0", "cB", "k", "q", "cA", "E1", "cfB", "qf", "v", "l0", "r0", "f0", "cfA", "kf", "l1", "r1", "t0", "f1", "t1",
-    "z1", "P0", "vf", "P1", "p0", "t2", "L1", "z0", "P2", "s0", "R1", "F0", "p1", "gA", "R0", "L0", "t3", "gB",
-    "s1", "F1", "P3", "a0", "a1", "dq", "p2", "p3", "s2", "gC", "dqf", "s3", "gD", "a2", "a3", "dk", "dv", "dql",
+    "cB", "E0", "q", "k", "E1", "qf", "r1", "cfB", "cA", "kf", "l1", "r0", "l0", "cfA", "P0", "t0", "f0", "v", "t1",
+    "f1", "z0", "p0", "vf", "z1", "t2", "P1", "L0", "F0", "p1", "s0", "R0", "P2", "t3", "R1", "L1", "s1", "gA",
+    "P3", "a0", "F1", "a1", "dq", "p2", "p3", "s2", "gB", "s3", "a2", "dqf", "a3", "dql", "dk", "gC", "dv", "dkf",
+    "dqlf", "gD", "dvf",
 ]
 
 
@@ -72,20 +74,6 @@
     dev_prev = (jnp.maximum(s - 1, 0), x, c)
     dev_next = (jnp.minimum(s + 1, 7), x, c)
 
-    barrier = pltpu.get_barrier_semaphore()
-    for dev in (dev_r, dev_l, dev_z, dev_a, dev_b):
-        pl.semaphore_signal(barrier, inc=1, device_id=dev, device_id_type=MESH)
-
-    @pl.when(has_prev)
-    def _():
-        pl.semaphore_signal(barrier, inc=1, device_id=dev_prev, device_id_type=MESH)
-
-    @pl.when(has_next)
-    def _():
-        pl.semaphore_signal(barrier, inc=1, device_id=dev_next, device_id_type=MESH)
-
-    pl.semaphore_wait(barrier, 5 + has_prev.astype(jnp.int32) + has_next.astype(jnp.int32))
-
     def m128(v):
         return pl.multiple_of(v, 128)
 
@@ -104,6 +92,36 @@
     in_pair = pl.ds(m128(HEAD * par), SLAB)
     in_pair_b = pl.ds(m128(HEAD * par_b), SLAB)
     own_full = pl.ds(m128(HEAD * par), HEAD)
+
+    def block(xx, start=0, size=ROWS):
+        half = xx // 2
+        return half, pl.ds(m128(ROWS * (xx - 2 * half) + start), size)
+
+    loads = []
+    for src, dst in (
+        (ks.at[0, :, own_slab], k2.at[(*block(x), in_pair)]),
+        (qs.at[0, :, own_slab], q2.at[(*block(x), in_pair)]),
+        (vs.at[0, :, own_slab], v2.at[(*block(x), in_pair)]),
+        (cx.at[0], ctx.at[x]),
+        (wo.at[0], wv),
+    ):
+        loads.append(pltpu.make_async_copy(src, dst, lsem.at[len(loads)]))
+    for copy in loads:
+        copy.start()
+
+    barrier = pltpu.get_barrier_semaphore()
+    for dev in (dev_r, dev_l, dev_z, dev_a, dev_b):
+        pl.semaphore_signal(barrier, inc=1, device_id=dev, device_id_type=MESH)
+
+    @pl.when(has_prev)
+    def _():
+        pl.semaphore_signal(barrier, inc=1, device_id=dev_prev, device_id_type=MESH)
+
+    @pl.when(has_next)
+    def _():
+        pl.semaphore_signal(barrier, inc=1, device_id=dev_next, device_id_type=MESH)
+
+    pl.semaphore_wait(barrier, 5 + has_prev.astype(jnp.int32) + has_next.astype(jnp.int32))
 
     def slot(yy, zz, q):
         return inc.at[zz, pl.ds(pl.multiple_of(PIECE * yy + CHUNK * q, CHUNK), CHUNK)]
@@ -129,10 +147,6 @@
             move("o_own%d" % q, slot(y_r, z, q), slot(y_r, z, q), slot(y_o, z, q), dev_l)
             move("o_oth%d" % q, slot(y_r, zp, q), slot(y_r, zp, q), slot(y_o, zp, q), dev_l)
 
-    def block(xx, start=0, size=ROWS):
-        half = xx // 2
-        return half, pl.ds(m128(ROWS * (xx - 2 * half) + start), size)
-
     for n, a, b in (("k", ks, k2), ("q", qs, q2), ("v", vs, v2)):
         to, from_a, from_b, from_c = block(x), block(x_a), block(x_b), block(x_c)
         move(n + "A", a.at[0, :, pair_of(x_a)], b.at[to], b.at[from_a], dev_a)
@@ -172,16 +186,6 @@
     def entry_kept(q):
         return pltpu.make_async_copy(bg.at[0, pl.ds(CHUNK * q, CHUNK)], slot(y, z, q), esem.at[q])
 
-    loads = []
-    for src, dst in (
-        (ks.at[0, :, own_slab], k2.at[(*block(x), in_pair)]),
-        (qs.at[0, :, own_slab], q2.at[(*block(x), in_pair)]),
-        (vs.at[0, :, own_slab], v2.at[(*block(x), in_pair)]),
-        (cx.at[0], ctx.at[x]),
-        (wo.at[0], wv),
-    ):
-        loads.append(pltpu.make_async_copy(src, dst, lsem.at[len(loads)]))
-
     def emit_send(tag):
         if tag[0] == "E":
             h = int(tag[1])
@@ -331,6 +335,9 @@
         "dk": ([], cast_keys, ["dk1", "dkA", "dkB"]),
         "dv": ([], cast_values, ["dv1", "dvA", "dvB"]),
         "dql": ([], None, ["dql1", "dqlA", "dqlB"]),
+        "dkf": (["dk1"], None, ["dkC"]),
+        "dvf": (["dv1"], None, ["dvC"]),
+        "dqlf": (["dql1"], None, ["dqlC"]),
         "gA": ([], lambda: weight_grad(0, 0), []),
         "gB": ([], lambda: weight_grad(0, 1), []),
         "gC": ([], lambda: weight_grad(1, 0), []),
@@ -377,12 +384,7 @@
                 emit_send(tag)
         for n, (b, g) in enumerate(((dqb, gq), (dkb, gk), (dvb, gv))):
             pltpu.make_async_copy(b.at[block(x)], g.at[0, :, own_slab], osem.at[n]).start()
-        for n in ("dk", "dv", "dql"):
-            emit_wait(n + "1")
-            emit_send(n + "C")
-
-    for copy in loads:
-        copy.start()
+
     for n, order in enumerate((ORDER0, ORDER1)):
         pl.when(core == n)(lambda order=order: perform(order))
 

time: 92.2 us -> 94.5 us (1.025)
  Pallas kernels: 91.3 us -> 93.3 us
    pallas_call x1, Pallas kernels: 88.7 us -> 90.7 us  [local(): pl.pallas_call(kernel, out_shape=[pltpu.VMEM(shape, BF16) for shape in sh...]
where the time goes in v4:
time: 94.5 us; the launch traced here: 94.1 us
  Pallas kernels  93.3 us (99%)
    pallas_call x1, Pallas kernels, local(): pl.pallas_call(kernel, out_shape=[pltpu.VMEM(shape, BF16) for shape in sh...  90.7 us
    pallas_call x1, Pallas kernels, local(): pl.pallas_call(write_out, out_shape=[jax.ShapeDtypeStruct(shape, BF16) fo...  2.62 us

profile of v4, /device:TPU:1, one launch (start us, length us, event | category | flops | bytes accessed | tf_op | source)
XLA Modules:
  0.0 94.1 jit_solution(2733249478377819219)
XLA Ops:
  0.6 90.7 %shard_map.93 = (bf16[1,768,3072]{2,1,0:T(8,128)(2,1)S(1)}, bf16[1,256,768]{2,1,0:T(8,128)(2,1)S(1)}, bf16[1,256,768]{2,1,0:T(8,128)(2,1)S(1)}, bf16[1,256,768]{2,1,0:T(8,128)(2,1)S(1)}) custom-call(bf16[1,128,3072]{2,1,0:T(8,128)(2,1)} %bg.1, bf16[1,768,3072]{2,1,0:T(8,128)(2,1)} %wo.1, bf16[1,256,768]{2,1,0:T(8,128)(2,1)} %cx.1, bf16[1,256,768]{2,1,0:T(8,128)(2,1)} %qs.1, ...), custom_call_target="tpu_custom_call" | custom-call | tf_op jit(solution)/shard_map/pallas_call | solution.py:426
  91.3 2.6 %shard_map.94 = (bf16[1,768,3072]{2,1,0:T(8,128)(2,1)}, bf16[1,256,768]{2,1,0:T(8,128)(2,1)}, bf16[1,256,768]{2,1,0:T(8,128)(2,1)}, bf16[1,256,768]{2,1,0:T(8,128)(2,1)}) custom-call(bf16[1,768,3072]{2,1,0:T(8,128)(2,1)S(1)} %get-tuple-element.8.gw, bf16[1,256,768]{2,1,0:T(8,128)(2,1)S(1)} %get-tuple-element.9.gq, ...), custom_call_target="tpu_custom_call" | custom-call | tf_op jit(solution)/shard_map/pallas_call | solution.py:467

commit v5 on v4

--- a/solution.py
+++ b/solution.py
@@ -24,16 +24,16 @@
 TILE = 512
 
 ORDER0 = [
-    "E1", "q", "r0", "k", "l0", "l1", "f0", "cB", "E0", "kf", "cA", "r1", "cfA", "f1", "z1", "cfB", "v", "z0", "p0",
-    "F0", "R1", "L1", "p1", "L0", "t0", "R0", "qf", "s0", "t1", "vf", "t2", "gA", "F1", "P0", "a0", "P1", "p2",
-    "s1", "P2", "p3", "gB", "s2", "P3", "a1", "dq", "s3", "a2", "dqf", "t3", "gC", "a3", "dql", "gD", "dk", "dqlf",
-    "dkf", "dv", "dvf",
+    "E0", "l0", "r0", "q", "cA", "l1", "f0", "E1", "qf", "k", "f1", "cB", "r1", "z1", "kf", "F0", "R1", "z0", "cfB",
+    "L1", "p0", "cfA", "v", "p1", "R0", "L0", "P0", "s0", "t0", "P1", "t1", "F1", "t2", "P2", "vf", "P3", "gA",
+    "s1", "p2", "gB", "a0", "p3", "p4", "s2", "a1", "t3", "dq", "s3", "s4", "gC", "a2", "dqf", "a3", "dk", "dv",
+    "dql", "gD", "dkf", "dvf", "dqlf",
 ]
 ORDER1 = [
-    "cB", "E0", "q", "k", "E1", "qf", "r1", "cfB", "cA", "kf", "l1", "r0", "l0", "cfA", "P0", "t0", "f0", "v", "t1",
-    "f1", "z0", "p0", "vf", "z1", "t2", "P1", "L0", "F0", "p1", "s0", "R0", "P2", "t3", "R1", "L1", "s1", "gA",
-    "P3", "a0", "F1", "a1", "dq", "p2", "p3", "s2", "gB", "s3", "a2", "dqf", "a3", "dql", "dk", "gC", "dv", "dkf",
-    "dqlf", "gD", "dvf",
+    "E0", "cB", "k", "q", "cA", "E1", "cfB", "qf", "v", "l0", "r0", "f0", "cfA", "kf", "l1", "r1", "t0", "f1", "t1",
+    "z1", "P0", "vf", "P1", "p0", "t2", "L1", "z0", "P2", "s0", "R1", "F0", "p1", "gA", "R0", "L0", "t3", "gB",
+    "s1", "F1", "P3", "a0", "a1", "dq", "p2", "p3", "p4", "s2", "gC", "dqf", "s3", "s4", "gD", "a2", "a3", "dk",
+    "dv", "dql", "dkf", "dvf", "dqlf",
 ]
 
 
@@ -44,7 +44,7 @@
 def kernel(
     bg, wo, cx, qs, ks, vs,
     gw, gq, gk, gv,
-    inc, wv, ctx, ctxt, acc, q2, k2, v2, qg, part, partb, got_a, got_b, sumb, kt, pt, linv, dout,
+    inc, wv, ctx, ctxt, acc, q2, k2, v2, qg, part, partb, got_a, got_b, sumb, part1, partb1, got_a1, got_b1, sumb1, kt, pt, linv, dout,
     dqa, dka, dva, dqb, dkb, dvb, stage,
     send, recv, lsem, esem, osem,
 ):
@@ -57,6 +57,7 @@
     y_r = lax.rem(y + 1 + 2 * core, 4)
     y_l = lax.rem(y + 3 + 2 * core, 4)
     y_o = lax.rem(y + 2, 4)
+    y_n = y_o + 1 - 2 * lax.rem(y_o, 2)
     zp = 1 - z
     pair = x // 2
     par = x - 2 * pair
@@ -133,6 +134,9 @@
     def move(tag, src, there, here, dev):
         moves[tag] = (len(moves), src, there, here, dev)
 
+    def sums_of(k):
+        return (partb, got_a, sumb, got_b) if k < 3 else (partb1, got_a1, sumb1, got_b1)
+
     for q in range(CHUNKS):
         move("E%d" % q, bg.at[0, pl.ds(CHUNK * q, CHUNK)], slot(y, z, q), slot(y, z, q), dev_prev)
         move("z%d" % q, slot(y, z, q), slot(y, z, q), slot(y, zp, q), dev_z)
@@ -157,9 +161,10 @@
     lo, hi = pl.ds(0, LOW), pl.ds(LOW, ROWS - LOW)
     move("cC0", ctx.at[x_a, lo], ctx.at[x_a, lo], ctx.at[x_c, lo], dev_b)
     move("cC1", ctx.at[x_b, hi], ctx.at[x_b, hi], ctx.at[x_c, hi], dev_a)
-    for k in range(4):
-        move("rsA%d" % k, partb.at[k, pair_of(x_a)], got_a.at[k], got_a.at[k], dev_a)
-        move("rsB%d" % k, sumb.at[k], got_b.at[k], got_b.at[k], dev_b)
+    for k in range(5):
+        src, first, total, second = (r.at[k] if k < 3 else r.at[k - 3] for r in (sums_of(k)))
+        move("rsA%d" % k, src.at[pair_of(x_a)], first, first, dev_a)
+        move("rsB%d" % k, total, second, second, dev_b)
 
     def move_out(n, src, dst, start, size, where):
         rows = pl.ds(start, size)
@@ -221,15 +226,23 @@
         return p, zz, pl.ds(m128(PIECE * zz), PIECE), pl.ds(m128(ROWS + PIECE * zz), PIECE)
 
     def partial_grad(k):
-        zz, p = groups[k]
-        tokens = pl.ds(pl.multiple_of(ROWS * p, ROWS), ROWS)
-        r = dot(wv[...], inc[zz, tokens], 1, 1)
-        part[k] = r
-        partb[k] = r.astype(BF16)
+        if k < 3:
+            zz, p = groups[k]
+            r = dot(wv[...], inc[zz, pl.ds(pl.multiple_of(ROWS * p, ROWS), ROWS)], 1, 1)
+            part[k] = r
+            partb[k] = r.astype(BF16)
+        else:
+            yy = (y_n, y_o)[k - 3]
+            r = dot(wv[...], inc[zp, pl.ds(m128(PIECE * yy), PIECE)], 1, 1)
+            part1[k - 3] = r
+            partb1[k - 3] = r.astype(BF16)
 
     def pass_on(k):
-        r = part[k, slab_of(x_b)] + got_a[k, in_pair_b].astype(F32)
-        sumb[k] = r.astype(BF16)
+        if k < 3:
+            sumb[k] = (part[k, slab_of(x_b)] + got_a[k, in_pair_b].astype(F32)).astype(BF16)
+        else:
+            i = k - 3
+            sumb1[i] = (part1[i, slab_of(x_b)] + got_a1[i, in_pair_b].astype(F32)).astype(BF16)
 
     heads = [pl.ds(HEAD * h, HEAD) for h in range(2)]
     pheads = [pl.ds(m128(HEAD * (par + h)), HEAD) for h in range(2)]
@@ -295,11 +308,14 @@
         if k == 0:
             dka[...] = jnp.zeros_like(dka)
             dva[...] = jnp.zeros_like(dva)
-        grad = part[k, own_slab] + got_a[k, in_pair].astype(F32) + got_b[k].astype(F32)
-        gb = grad.astype(BF16)
-        dout[...] = gb
+        if k < 3:
+            dout[...] = (part[k, own_slab] + got_a[k, in_pair].astype(F32) + got_b[k].astype(F32)).astype(BF16)
+        else:
+            for i, yy in enumerate((y_n, y_o)):
+                r = part1[i, own_slab] + got_a1[i, in_pair].astype(F32) + got_b1[i].astype(F32)
+                dout[:, pl.ds(m128(PIECE * lax.rem(yy, 2)), PIECE)] = r.astype(BF16)
         tokens = pl.ds(pl.multiple_of(ROWS * p, ROWS), ROWS)
-        prod = gb.astype(F32) * ctxt[k // 2, own_slab, tokens].astype(F32)
+        prod = dout[...].astype(F32) * ctxt[k // 2, own_slab, tokens].astype(F32)
         deltas = [jnp.sum(prod[HEAD * h : HEAD * (h + 1)], axis=0, keepdims=True) for h in range(2)]
         inv = [linv[k, h : h + 1] for h in range(2)]
         dqa[...] = jnp.zeros_like(dqa)
@@ -363,12 +379,14 @@
         far += ["o_own" + i]
         near_z += ["z" + i, "l_oth" + i, "r_oth" + i]
         far_z += ["o_oth" + i]
-    for k, need in enumerate((["@4"] + own + near, far, near_z, far_z)):
+    for k, need in enumerate((["@4"] + own + near, far, near_z, near_z, far_z)):
         table["p%d" % k] = (need, lambda k=k: partial_grad(k), ["rsA%d" % k])
         table["s%d" % k] = (["rsA%d" % k], lambda k=k: pass_on(k), ["rsB%d" % k])
+    for k in range(4):
+        sums = ["rsB%d" % k] if k < 3 else ["rsB3", "rsB4"]
         table["P%d" % k] = (["@0", "@1", "kA", "kB", "kC", "qA", "qB", "qC"], lambda k=k: softmax(k), [])
         table["t%d" % k] = (["@3", "cA", "cB", "cC0", "cC1"], lambda k=k: turn(k), [])
-        table["a%d" % k] = (["@2", "vA", "vB", "vC", "rsB%d" % k], lambda k=k: attend(k), [])
+        table["a%d" % k] = (["@2", "vA", "vB", "vC"] + sums, lambda k=k: attend(k), [])
 
     def perform(order):
         seen = set()
@@ -403,7 +421,7 @@
             outgoing(tag).wait_send()
 
 
-N_MOVES = 8 * CHUNKS + 9 + 4 + 8 + 16
+N_MOVES = 8 * CHUNKS + 9 + 4 + 10 + 16
 
 
 def write_out(gw, gq, gk, gv, gw_out, gq_out, gk_out, gv_out, sems):
@@ -438,11 +456,16 @@
             pltpu.VMEM((2, KEYS, PAIR), BF16),
             pltpu.VMEM((2, KEYS, PAIR), BF16),
             pltpu.VMEM((4, ROWS, SLAB), BF16),
-            pltpu.VMEM((4, WIDTH, ROWS), F32),
-            pltpu.VMEM((4, WIDTH, ROWS), BF16),
-            pltpu.VMEM((4, PAIR, ROWS), BF16),
-            pltpu.VMEM((4, SLAB, ROWS), BF16),
-            pltpu.VMEM((4, SLAB, ROWS), BF16),
+            pltpu.VMEM((3, WIDTH, ROWS), F32),
+            pltpu.VMEM((3, WIDTH, ROWS), BF16),
+            pltpu.VMEM((3, PAIR, ROWS), BF16),
+            pltpu.VMEM((3, SLAB, ROWS), BF16),
+            pltpu.VMEM((3, SLAB, ROWS), BF16),
+            pltpu.VMEM((2, WIDTH, PIECE), F32),
+            pltpu.VMEM((2, WIDTH, PIECE), BF16),
+            pltpu.VMEM((2, PAIR, PIECE), BF16),
+            pltpu.VMEM((2, SLAB, PIECE), BF16),
+            pltpu.VMEM((2, SLAB, PIECE), BF16),
             pltpu.VMEM((2, SLAB, KEYS), BF16),
             pltpu.VMEM((2, 4, 2, KEYS, ROWS), F32),
             pltpu.VMEM((4, 8, ROWS), F32),

time: 94.5 us -> 92.6 us (0.980)
  Pallas kernels: 93.3 us -> 91.7 us
    pallas_call x1, Pallas kernels: 90.7 us -> 89.1 us  [local(): pl.pallas_call(kernel, out_shape=[pltpu.VMEM(shape, BF16) for shape in sh...]
where the time goes in v5:
time: 92.6 us; the launch traced here: 92.5 us
  Pallas kernels  91.7 us (99%)
    pallas_call x1, Pallas kernels, local(): pl.pallas_call(kernel, out_shape=[pltpu.VMEM(shape, BF16) for shape in sh...  89.1 us
    pallas_call x1, Pallas kernels, local(): pl.pallas_call(write_out, out_shape=[jax.ShapeDtypeStruct(shape, BF16) fo...  2.62 us

profile of v5, /device:TPU:1, one launch (start us, length us, event | category | flops | bytes accessed | tf_op | source)
XLA Modules:
  0.0 92.5 jit_solution(16848763756180341673)
XLA Ops:
  0.6 89.1 %shard_map.93 = (bf16[1,768,3072]{2,1,0:T(8,128)(2,1)S(1)}, bf16[1,256,768]{2,1,0:T(8,128)(2,1)S(1)}, bf16[1,256,768]{2,1,0:T(8,128)(2,1)S(1)}, bf16[1,256,768]{2,1,0:T(8,128)(2,1)S(1)}) custom-call(bf16[1,128,3072]{2,1,0:T(8,128)(2,1)} %bg.1, bf16[1,768,3072]{2,1,0:T(8,128)(2,1)} %wo.1, bf16[1,256,768]{2,1,0:T(8,128)(2,1)} %cx.1, bf16[1,256,768]{2,1,0:T(8,128)(2,1)} %qs.1, ...), custom_call_target="tpu_custom_call" | custom-call | tf_op jit(solution)/shard_map/pallas_call | solution.py:444
  89.8 2.6 %shard_map.94 = (bf16[1,768,3072]{2,1,0:T(8,128)(2,1)}, bf16[1,256,768]{2,1,0:T(8,128)(2,1)}, bf16[1,256,768]{2,1,0:T(8,128)(2,1)}, bf16[1,256,768]{2,1,0:T(8,128)(2,1)}) custom-call(bf16[1,768,3072]{2,1,0:T(8,128)(2,1)S(1)} %get-tuple-element.8.gw, bf16[1,256,768]{2,1,0:T(8,128)(2,1)S(1)} %get-tuple-element.9.gq, ...), custom_call_target="tpu_custom_call" | custom-call | tf_op jit(solution)/shard_map/pallas_call | solution.py:490

commit v6 on v5

--- a/solution.py
+++ b/solution.py
@@ -7,6 +7,7 @@
 
 HEAD = 128
 SCALE = HEAD ** (-0.5)
+EXP_SCALE = SCALE * 1.4426950408889634
 MESH = pl.DeviceIdType.MESH
 BF16 = jnp.bfloat16
 F32 = jnp.float32
@@ -24,17 +25,18 @@
 TILE = 512
 
 ORDER0 = [
-    "E0", "l0", "r0", "q", "cA", "l1", "f0", "E1", "qf", "k", "f1", "cB", "r1", "z1", "kf", "F0", "R1", "z0", "cfB",
-    "L1", "p0", "cfA", "v", "p1", "R0", "L0", "P0", "s0", "t0", "P1", "t1", "F1", "t2", "P2", "vf", "P3", "gA",
-    "s1", "p2", "gB", "a0", "p3", "p4", "s2", "a1", "t3", "dq", "s3", "s4", "gC", "a2", "dqf", "a3", "dk", "dv",
-    "dql", "gD", "dkf", "dvf", "dqlf",
+    "cB", "E0", "cA", "k", "l1", "r0", "r1", "l0", "E1", "f1", "f0", "v", "p0", "z1", "cfB", "cfA", "z0", "t0",
+    "t1", "q", "F0", "kf", "t2", "R1", "L1", "p1", "gA", "L0", "qf", "s0", "gB", "vf", "R0", "s1", "F1", "P0", "P1",
+    "P2", "p2", "t3", "P3", "p3", "p4", "a0", "s2", "s3", "s4", "a1", "a2", "dq", "a3", "dqf", "dk", "dv", "dql",
+    "sent", "gC", "dkf", "dqlf", "dvf", "gD",
 ]
 ORDER1 = [
-    "E0", "cB", "k", "q", "cA", "E1", "cfB", "qf", "v", "l0", "r0", "f0", "cfA", "kf", "l1", "r1", "t0", "f1", "t1",
-    "z1", "P0", "vf", "P1", "p0", "t2", "L1", "z0", "P2", "s0", "R1", "F0", "p1", "gA", "R0", "L0", "t3", "gB",
-    "s1", "F1", "P3", "a0", "a1", "dq", "p2", "p3", "p4", "s2", "gC", "dqf", "s3", "s4", "gD", "a2", "a3", "dk",
-    "dv", "dql", "dkf", "dvf", "dqlf",
+    "E1", "q", "cB", "k", "v", "E0", "kf", "cA", "r0", "l0", "cfB", "qf", "l1", "r1", "P0", "f0", "z1", "P1", "cfA",
+    "z0", "f1", "P2", "p0", "P3", "t0", "t1", "s0", "t2", "F0", "p1", "L1", "vf", "R0", "gA", "L0", "R1", "a0",
+    "s1", "gB", "F1", "a1", "dq", "p2", "p3", "p4", "s2", "t3", "s3", "s4", "dqf", "a2", "a3", "dql", "dv", "dk",
+    "gC", "sent", "dvf", "dqlf", "gD", "dkf",
 ]
+LAST = ("dk", "dv", "dq")
 
 
 def dot(a, b, ca, cb):
@@ -264,7 +266,7 @@
             result = []
             ok = ahead >= KEYS * (j - p) - PIECE * zz
             for h in range(2):
-                sc = dot(k2[j, :, pheads[h]], qg[k, :, heads[h]], 1, 1) * SCALE
+                sc = dot(k2[j, :, pheads[h]], qg[k, :, heads[h]], 1, 1)
                 sc = jnp.where(ok, sc, -jnp.inf)
                 pt[h, k, j] = sc
                 result.append(jnp.maximum(tops[h], jnp.max(sc, axis=0, keepdims=True)))
@@ -276,7 +278,7 @@
         def weights(j, sums):
             result = []
             for h in range(2):
-                e = jnp.exp(pt[h, k, j] - tops[h])
+                e = jnp.exp2((pt[h, k, j] - tops[h]) * EXP_SCALE)
                 pt[h, k, j] = e
                 result.append(sums[h] + jnp.sum(e, axis=0, keepdims=True))
             return tuple(result)
@@ -341,6 +343,16 @@
     def cast_values():
         dvb[...] = dva[...].astype(BF16)
 
+    def early_sent():
+        for tag in moves:
+            if tag[0] == "E":
+
+                @pl.when(has_prev)
+                def _():
+                    outgoing(tag).wait_send()
+            elif tag[:2] not in LAST:
+                outgoing(tag).wait_send()
+
     table = {
         "cA": ([], None, ["cA"]),
         "cB": ([], None, ["cB"]),
@@ -351,6 +363,7 @@
         "dk": ([], cast_keys, ["dk1", "dkA", "dkB"]),
         "dv": ([], cast_values, ["dv1", "dvA", "dvB"]),
         "dql": ([], None, ["dql1", "dqlA", "dqlB"]),
+        "sent": ([], early_sent, []),
         "dkf": (["dk1"], None, ["dkC"]),
         "dvf": (["dv1"], None, ["dvC"]),
         "dqlf": (["dql1"], None, ["dqlC"]),
@@ -412,12 +425,7 @@
     for n, (b, g) in enumerate(((dqb, gq), (dkb, gk), (dvb, gv))):
         pltpu.make_async_copy(b.at[block(x)], g.at[0, :, own_slab], osem.at[n]).wait()
     for tag in moves:
-        if tag[0] == "E":
-
-            @pl.when(has_prev)
-            def _():
-                outgoing(tag).wait_send()
-        else:
+        if tag[:2] in LAST:
             outgoing(tag).wait_send()
 
 

time: 92.6 us -> 91.9 us (level); the launches traced: 92.5 us -> 90.9 us
  Pallas kernels: 91.7 us -> 90 us
    pallas_call x1, Pallas kernels: 89.1 us -> 87.4 us  [local(): pl.pallas_call(kernel, out_shape=[pltpu.VMEM(shape, BF16) for shape in sh...]
where the time goes in v6:
time: 91.9 us; the launch traced here: 90.9 us
  Pallas kernels  90 us (98%)
    pallas_call x1, Pallas kernels, local(): pl.pallas_call(kernel, out_shape=[pltpu.VMEM(shape, BF16) for shape in sh...  87.4 us
    pallas_call x1, Pallas kernels, local(): pl.pallas_call(write_out, out_shape=[jax.ShapeDtypeStruct(shape, BF16) fo...  2.62 us

profile of v6, /device:TPU:1, one launch (start us, length us, event | category | flops | bytes accessed | tf_op | source)
XLA Modules:
  0.0 90.9 jit_solution(6538208861843496677)
XLA Ops:
  0.6 87.4 %shard_map.93 = (bf16[1,768,3072]{2,1,0:T(8,128)(2,1)S(1)}, bf16[1,256,768]{2,1,0:T(8,128)(2,1)S(1)}, bf16[1,256,768]{2,1,0:T(8,128)(2,1)S(1)}, bf16[1,256,768]{2,1,0:T(8,128)(2,1)S(1)}) custom-call(bf16[1,128,3072]{2,1,0:T(8,128)(2,1)} %bg.1, bf16[1,768,3072]{2,1,0:T(8,128)(2,1)} %wo.1, bf16[1,256,768]{2,1,0:T(8,128)(2,1)} %cx.1, bf16[1,256,768]{2,1,0:T(8,128)(2,1)} %qs.1, ...), custom_call_target="tpu_custom_call" | custom-call | tf_op jit(solution)/shard_map/pallas_call | solution.py:452
  88.1 2.6 %shard_map.94 = (bf16[1,768,3072]{2,1,0:T(8,128)(2,1)}, bf16[1,256,768]{2,1,0:T(8,128)(2,1)}, bf16[1,256,768]{2,1,0:T(8,128)(2,1)}, bf16[1,256,768]{2,1,0:T(8,128)(2,1)}) custom-call(bf16[1,768,3072]{2,1,0:T(8,128)(2,1)S(1)} %get-tuple-element.8.gw, bf16[1,256,768]{2,1,0:T(8,128)(2,1)S(1)} %get-tuple-element.9.gq, ...), custom_call_target="tpu_custom_call" | custom-call | tf_op jit(solution)/shard_map/pallas_call | solution.py:498

commit v7 on v6

--- a/solution.py
+++ b/solution.py
@@ -116,15 +116,13 @@
     for dev in (dev_r, dev_l, dev_z, dev_a, dev_b):
         pl.semaphore_signal(barrier, inc=1, device_id=dev, device_id_type=MESH)
 
-    @pl.when(has_prev)
-    def _():
-        pl.semaphore_signal(barrier, inc=1, device_id=dev_prev, device_id_type=MESH)
-
     @pl.when(has_next)
     def _():
         pl.semaphore_signal(barrier, inc=1, device_id=dev_next, device_id_type=MESH)
 
-    pl.semaphore_wait(barrier, 5 + has_prev.astype(jnp.int32) + has_next.astype(jnp.int32))
+    dka[...] = jnp.zeros_like(dka)
+    dva[...] = jnp.zeros_like(dva)
+    pl.semaphore_wait(barrier, 5 + has_prev.astype(jnp.int32))
 
     def slot(yy, zz, q):
         return inc.at[zz, pl.ds(pl.multiple_of(PIECE * yy + CHUNK * q, CHUNK), CHUNK)]
@@ -307,9 +305,6 @@
 
     def attend(k):
         p, _, rows0, rows1 = group_rows(groups[k])
-        if k == 0:
-            dka[...] = jnp.zeros_like(dka)
-            dva[...] = jnp.zeros_like(dva)
         if k < 3:
             dout[...] = (part[k, own_slab] + got_a[k, in_pair].astype(F32) + got_b[k].astype(F32)).astype(BF16)
         else:

time: 91.9 us -> 93.3 us (1.015)
  the two profiles are of different devices: /device:TPU:1 before, /device:TPU:89 now
where the time goes in v7:
time: 93.3 us; the launch traced here: 93.2 us
  Pallas kernels  92.4 us (99%)
    pallas_call x1, Pallas kernels, local(): pl.pallas_call(kernel, out_shape=[pltpu.VMEM(shape, BF16) for shape in sh...  89.8 us
    pallas_call x1, Pallas kernels, local(): pl.pallas_call(write_out, out_shape=[jax.ShapeDtypeStruct(shape, BF16) fo...  2.62 us

profile of v7, /device:TPU:89, one launch (start us, length us, event | category | flops | bytes accessed | tf_op | source)
XLA Modules:
  0.0 93.2 jit_solution(7807570253565187398)
XLA Ops:
  0.6 89.8 %shard_map.93 = (bf16[1,768,3072]{2,1,0:T(8,128)(2,1)S(1)}, bf16[1,256,768]{2,1,0:T(8,128)(2,1)S(1)}, bf16[1,256,768]{2,1,0:T(8,128)(2,1)S(1)}, bf16[1,256,768]{2,1,0:T(8,128)(2,1)S(1)}) custom-call(bf16[1,128,3072]{2,1,0:T(8,128)(2,1)} %bg.1, bf16[1,768,3072]{2,1,0:T(8,128)(2,1)} %wo.1, bf16[1,256,768]{2,1,0:T(8,128)(2,1)} %cx.1, bf16[1,256,768]{2,1,0:T(8,128)(2,1)} %qs.1, ...), custom_call_target="tpu_custom_call" | custom-call | tf_op jit(solution)/shard_map/pallas_call | solution.py:447
  90.4 2.6 %shard_map.94 = (bf16[1,768,3072]{2,1,0:T(8,128)(2,1)}, bf16[1,256,768]{2,1,0:T(8,128)(2,1)}, bf16[1,256,768]{2,1,0:T(8,128)(2,1)}, bf16[1,256,768]{2,1,0:T(8,128)(2,1)}) custom-call(bf16[1,768,3072]{2,1,0:T(8,128)(2,1)S(1)} %get-tuple-element.8.gw, bf16[1,256,768]{2,1,0:T(8,128)(2,1)S(1)} %get-tuple-element.9.gq, ...), custom_call_target="tpu_custom_call" | custom-call | tf_op jit(solution)/shard_map/pallas_call | solution.py:493

commit v8 on v7

--- a/solution.py
+++ b/solution.py
@@ -27,14 +27,14 @@
 ORDER0 = [
     "cB", "E0", "cA", "k", "l1", "r0", "r1", "l0", "E1", "f1", "f0", "v", "p0", "z1", "cfB", "cfA", "z0", "t0",
     "t1", "q", "F0", "kf", "t2", "R1", "L1", "p1", "gA", "L0", "qf", "s0", "gB", "vf", "R0", "s1", "F1", "P0", "P1",
-    "P2", "p2", "t3", "P3", "p3", "p4", "a0", "s2", "s3", "s4", "a1", "a2", "dq", "a3", "dqf", "dk", "dv", "dql",
-    "sent", "gC", "dkf", "dqlf", "dvf", "gD",
+    "P2", "p2", "t3", "P3", "p3", "p4", "a0", "s2", "s3", "s4", "a1", "a2", "dq", "a3", "dk", "dv", "dql",
+    "sent", "gC", "gD",
 ]
 ORDER1 = [
     "E1", "q", "cB", "k", "v", "E0", "kf", "cA", "r0", "l0", "cfB", "qf", "l1", "r1", "P0", "f0", "z1", "P1", "cfA",
     "z0", "f1", "P2", "p0", "P3", "t0", "t1", "s0", "t2", "F0", "p1", "L1", "vf", "R0", "gA", "L0", "R1", "a0",
-    "s1", "gB", "F1", "a1", "dq", "p2", "p3", "p4", "s2", "t3", "s3", "s4", "dqf", "a2", "a3", "dql", "dv", "dk",
-    "gC", "sent", "dvf", "dqlf", "gD", "dkf",
+    "s1", "gB", "F1", "a1", "dq", "p2", "p3", "p4", "s2", "t3", "s3", "s4", "a2", "a3", "dql", "dv", "dk",
+    "gC", "sent", "gD",
 ]
 LAST = ("dk", "dv", "dq")
 
@@ -47,7 +47,7 @@
     bg, wo, cx, qs, ks, vs,
     gw, gq, gk, gv,
     inc, wv, ctx, ctxt, acc, q2, k2, v2, qg, part, partb, got_a, got_b, sumb, part1, partb1, got_a1, got_b1, sumb1, kt, pt, linv, dout,
-    dqa, dka, dva, dqb, dkb, dvb, stage,
+    dqa, dka, dva, dqb, dkb, dvb,
     send, recv, lsem, esem, osem,
 ):
     s = lax.axis_index("section")
@@ -72,6 +72,7 @@
     dev_z = (s, x, 2 * y + zp)
     dev_a = (s, x_a, c)
     dev_b = (s, x_b, c)
+    dev_c = (s, x_c, c)
     has_prev = s > 0
     has_next = s < 7
     dev_prev = (jnp.maximum(s - 1, 0), x, c)
@@ -113,7 +114,7 @@
         copy.start()
 
     barrier = pltpu.get_barrier_semaphore()
-    for dev in (dev_r, dev_l, dev_z, dev_a, dev_b):
+    for dev in (dev_r, dev_l, dev_z, dev_a, dev_b, dev_c):
         pl.semaphore_signal(barrier, inc=1, device_id=dev, device_id_type=MESH)
 
     @pl.when(has_next)
@@ -122,7 +123,7 @@
 
     dka[...] = jnp.zeros_like(dka)
     dva[...] = jnp.zeros_like(dva)
-    pl.semaphore_wait(barrier, 5 + has_prev.astype(jnp.int32))
+    pl.semaphore_wait(barrier, 6 + has_prev.astype(jnp.int32))
 
     def slot(yy, zz, q):
         return inc.at[zz, pl.ds(pl.multiple_of(PIECE * yy + CHUNK * q, CHUNK), CHUNK)]
@@ -166,19 +167,17 @@
         move("rsA%d" % k, src.at[pair_of(x_a)], first, first, dev_a)
         move("rsB%d" % k, total, second, second, dev_b)
 
-    def move_out(n, src, dst, start, size, where):
+    def move_out(n, src, dst, start, size):
         rows = pl.ds(start, size)
-        hop = stage.at[where, pl.ds(0, size)]
         to_a, to_b, to_c = (block(xx, start, size) for xx in (x_a, x_b, x_c))
-        move(n + "1", src.at[(*to_c, own_full)], hop, hop, dev_b)
         move(n + "A", src.at[to_a], dst.at[0, rows, own_slab], dst.at[0, rows, slab_of(x_a)], dev_a)
         move(n + "B", src.at[(*to_b, own_full)], dst.at[0, rows, full_of(x)], dst.at[0, rows, full_of(x_b)], dev_b)
-        move(n + "C", hop, dst.at[0, rows, full_of(x_b)], dst.at[0, rows, full_of(x_c)], dev_a)
-
-    move_out("dk", dkb, gk, 0, ROWS, 0)
-    move_out("dv", dvb, gv, 0, ROWS, 1)
-    move_out("dqe", dqb, gq, m128(PIECE * z), PIECE, 2)
-    move_out("dql", dqb, gq, m128(PIECE * zp), PIECE, 3)
+        move(n + "C", src.at[(*to_c, own_full)], dst.at[0, rows, full_of(x)], dst.at[0, rows, full_of(x_c)], dev_c)
+
+    move_out("dk", dkb, gk, 0, ROWS)
+    move_out("dv", dvb, gv, 0, ROWS)
+    move_out("dqe", dqb, gq, m128(PIECE * z), PIECE)
+    move_out("dql", dqb, gq, m128(PIECE * zp), PIECE)
 
     def outgoing(tag):
         i, src, there, _, dev = moves[tag]
@@ -353,15 +352,11 @@
         "cB": ([], None, ["cB"]),
         "cfA": (["cA"], None, ["cC0"]),
         "cfB": (["cB"], None, ["cC1"]),
-        "dq": ([], None, ["dqe1", "dqeA", "dqeB"]),
-        "dqf": (["dqe1"], None, ["dqeC"]),
-        "dk": ([], cast_keys, ["dk1", "dkA", "dkB"]),
-        "dv": ([], cast_values, ["dv1", "dvA", "dvB"]),
-        "dql": ([], None, ["dql1", "dqlA", "dqlB"]),
+        "dq": ([], None, ["dqeC", "dqeA", "dqeB"]),
+        "dk": ([], cast_keys, ["dkC", "dkA", "dkB"]),
+        "dv": ([], cast_values, ["dvC", "dvA", "dvB"]),
+        "dql": ([], None, ["dqlC", "dqlA", "dqlB"]),
         "sent": ([], early_sent, []),
-        "dkf": (["dk1"], None, ["dkC"]),
-        "dvf": (["dv1"], None, ["dvC"]),
-        "dqlf": (["dql1"], None, ["dqlC"]),
         "gA": ([], lambda: weight_grad(0, 0), []),
         "gB": ([], lambda: weight_grad(0, 1), []),
         "gC": ([], lambda: weight_grad(1, 0), []),
@@ -424,7 +419,7 @@
             outgoing(tag).wait_send()
 
 
-N_MOVES = 8 * CHUNKS + 9 + 4 + 10 + 16
+N_MOVES = 8 * CHUNKS + 9 + 4 + 10 + 12
 
 
 def write_out(gw, gq, gk, gv, gw_out, gq_out, gk_out, gv_out, sems):
@@ -479,7 +474,6 @@
             pltpu.VMEM((2, KEYS, SLAB), BF16),
             pltpu.VMEM((2, KEYS, SLAB), BF16),
             pltpu.VMEM((2, KEYS, SLAB), BF16),
-            pltpu.VMEM((4, ROWS, HEAD), BF16),
             pltpu.SemaphoreType.DMA((N_MOVES,)),
             pltpu.SemaphoreType.DMA((N_MOVES,)),
             pltpu.SemaphoreType.DMA((5,)),

time: 93.3 us -> 91.5 us (0.981)
  the two profiles are of different devices: /device:TPU:89 before, /device:TPU:73 now
where the time goes in v8:
time: 91.5 us; the launch traced here: 91.4 us
  Pallas kernels  90.6 us (99%)
    pallas_call x1, Pallas kernels, local(): pl.pallas_call(kernel, out_shape=[pltpu.VMEM(shape, BF16) for shape in sh...  88 us
    pallas_call x1, Pallas kernels, local(): pl.pallas_call(write_out, out_shape=[jax.ShapeDtypeStruct(shape, BF16) fo...  2.62 us

profile of v8, /device:TPU:73, one launch (start us, length us, event | category | flops | bytes accessed | tf_op | source)
XLA Modules:
  0.0 91.4 jit_solution(9910822824072561923)
XLA Ops:
  0.6 88.0 %shard_map.93 = (bf16[1,768,3072]{2,1,0:T(8,128)(2,1)S(1)}, bf16[1,256,768]{2,1,0:T(8,128)(2,1)S(1)}, bf16[1,256,768]{2,1,0:T(8,128)(2,1)S(1)}, bf16[1,256,768]{2,1,0:T(8,128)(2,1)S(1)}) custom-call(bf16[1,128,3072]{2,1,0:T(8,128)(2,1)} %bg.1, bf16[1,768,3072]{2,1,0:T(8,128)(2,1)} %wo.1, bf16[1,256,768]{2,1,0:T(8,128)(2,1)} %cx.1, bf16[1,256,768]{2,1,0:T(8,128)(2,1)} %qs.1, ...), custom_call_target="tpu_custom_call" | custom-call | tf_op jit(solution)/shard_map/pallas_call | solution.py:442
  88.6 2.6 %shard_map.94 = (bf16[1,768,3072]{2,1,0:T(8,128)(2,1)}, bf16[1,256,768]{2,1,0:T(8,128)(2,1)}, bf16[1,256,768]{2,1,0:T(8,128)(2,1)}, bf16[1,256,768]{2,1,0:T(8,128)(2,1)}) custom-call(bf16[1,768,3072]{2,1,0:T(8,128)(2,1)S(1)} %get-tuple-element.8.gw, bf16[1,256,768]{2,1,0:T(8,128)(2,1)S(1)} %get-tuple-element.9.gq, ...), custom_call_target="tpu_custom_call" | custom-call | tf_op jit(solution)/shard_map/pallas_call | solution.py:487
